TPU v7x, 512 devices: a whole 4x8x8 slice. The times are simulated.
512 devices in a mesh: seq: 64 (over x, z, core), tensor: 8 (over y).
Axes of the slice: x: 4, y: 8, z: 8, core: 2. Of those that a mesh axis runs over, the one named last changes fastest.
Arguments:
- queries: bfloat16 [8192, 12288], P(('seq', 'tensor')), may hold values from -5 to 5
- keys: bfloat16 [8192, 1024], P(('seq', 'tensor')), may hold values from -5 to 5
- values: bfloat16 [8192, 1024], P(('seq', 'tensor')), may hold values from -6 to 6
- tile_len: int32 [64], replicated, may hold values from 2 to 128, as said below
- ancestors: int32 [64, 52], P('seq'), may hold values from -1 to 62, as said below
Outputs:
- attended: bfloat16 [8192, 12288], P(('seq', 'tensor'))
Inputs may be any that keep to these rules, and one draw needn't show every extreme that they name: `tile_len`: some tile is full. `ancestors`: the shards form a tree: shard 0 is the root; the list of shard s is its parent's list followed by the parent's first tile (tile number p, since 1 = 1), where the parent p is an earlier shard; entries are ordered from the root and padded at the end with -1; some shard lists exactly 52 tiles.
All inputs are finite; a program needn't handle non-finite values.
Results may differ from a plain program's by a relative error of at most 0.0065.
Values may be sent and summed in bfloat16 or wider, within the bound.
No kernel may reach another device: no remote copies, remote signals or barrier semaphores. Data moves between devices by JAX's collectives and lax.ppermute only.
A program may use at most 64 MiB of HBM per device.

v0:
```python
import math

import jax
import jax.numpy as jnp
from jax import lax
from jax.sharding import PartitionSpec as P

HEADS = 96
KV = 8
HD = 128
TILE = 128
TILE_DEV = 1


def local(queries, keys, values, tile_len, ancestors):
    q_heads, k_heads, v_heads = (
        lax.all_to_all(queries, "tensor", split_axis=1, concat_axis=0, tiled=True),
        lax.all_to_all(keys, "tensor", split_axis=1, concat_axis=0, tiled=True),
        lax.all_to_all(values, "tensor", split_axis=1, concat_axis=0, tiled=True),
    )
    tok_count = q_heads.shape[0]
    kv_local = k_heads.shape[1] // HD
    per_group = HEADS // KV
    query_four = q_heads.reshape(tok_count, kv_local, per_group, HD)
    scaling = 1.0 / math.sqrt(HD)

    def attend(carry_state, block_rows, mask):
        maxima, totals, summed = carry_state
        half_width = block_rows.shape[1] // 2
        key_count = block_rows.shape[0]
        key_block = block_rows[:, :half_width].reshape(key_count, kv_local, HD)
        val_block = block_rows[:, half_width:].reshape(key_count, kv_local, HD)
        scores = (
            jnp.einsum("igrd,kgd->grik", query_four, key_block, preferred_element_type=jnp.float32)
            * scaling
        )
        scores = jnp.where(mask, scores, -1e30)
        running_max = jnp.maximum(maxima, jnp.max(scores, axis=-1))
        weights = jnp.exp(scores - running_max[..., None]).astype(jnp.bfloat16)
        factor = jnp.exp(maxima - running_max)
        totals = totals * factor + jnp.sum(weights, axis=-1, dtype=jnp.float32)
        summed = summed * jnp.moveaxis(factor, 2, 0)[..., None] + jnp.einsum(
            "grik,kgd->igrd", weights, val_block, preferred_element_type=jnp.float32
        )
        return (running_max, totals, summed)

    kv_rows = jnp.concatenate([k_heads, v_heads], axis=1)
    offsets = jnp.arange(tok_count, dtype=jnp.int32)
    seq_index = lax.axis_index("seq")
    own_len = lax.dynamic_slice_in_dim(tile_len, seq_index * TILE_DEV, TILE_DEV)
    own_valid = offsets % TILE < jnp.repeat(own_len, TILE, total_repeat_length=tok_count)
    near_mask = own_valid[None, :] & (offsets[None, :] <= offsets[:, None])
    start_state = (
        jnp.full((kv_local, per_group, tok_count), -1e30, jnp.float32),
        jnp.zeros((kv_local, per_group, tok_count), jnp.float32),
        jnp.zeros((tok_count, kv_local, per_group, HD), jnp.float32),
    )
    carry_state = attend(start_state, kv_rows, near_mask)
    listed = ancestors[0]
    tile_count = tile_len.shape[0]
    owners = jnp.arange(lax.axis_size("seq"), dtype=jnp.int32)
    wanted = (
        jnp.any(listed[None, :] == TILE_DEV * owners[:, None], axis=1)
        .astype(jnp.int32)
        .reshape(-1, 1)
    )
    asked_for = lax.all_to_all(wanted, "seq", split_axis=0, concat_axis=0, tiled=True)
    outgoing = jnp.where(asked_for[:, :, None] > 0, kv_rows[None], jnp.zeros_like(kv_rows)[None])
    fetched = lax.all_to_all(outgoing, "seq", split_axis=0, concat_axis=0, tiled=True)
    safe_ids = jnp.maximum(listed, 0)
    chosen = jnp.take(fetched, safe_ids // TILE_DEV, axis=0)
    far_len = jnp.sum(
        jnp.where(
            safe_ids[:, None] == jnp.arange(tile_count, dtype=jnp.int32)[None, :],
            tile_len[None, :],
            0,
        ),
        axis=1,
    )
    far_mask = (listed[:, None] >= 0) & (
        jnp.arange(TILE, dtype=jnp.int32)[None, :] < far_len[:, None]
    )
    depth = listed.shape[0]
    paired = chosen.reshape(depth // 2, 2 * TILE, chosen.shape[2])
    paired_mask = far_mask.reshape(depth // 2, 2 * TILE)

    def step_pair(inner_state, pair):
        return (attend(inner_state, pair[0], pair[1]), None)

    carry_state, unused = lax.scan(step_pair, carry_state, (paired, paired_mask))
    maxima, totals, summed = carry_state
    result = (summed / jnp.moveaxis(totals, 2, 0)[..., None]).astype(jnp.bfloat16)
    result = result.reshape(tok_count, kv_local * per_group * HD)
    return lax.all_to_all(result, "tensor", split_axis=0, concat_axis=1, tiled=True)


def solution(mesh):
    in_specs = (
        P(("seq", "tensor"), None),
        P(("seq", "tensor"), None),
        P(("seq", "tensor"), None),
        P(),
        P("seq", None),
    )
    out_specs = P(("seq", "tensor"), None)
    return jax.shard_map(local, mesh=mesh, in_specs=in_specs, out_specs=out_specs, check_vma=False)
```

profile of v0, /device:TPU:6, one launch (start us, length us, event | category | flops | bytes accessed | tf_op | source)
XLA Modules:
  0.0 251.6 jit_solution(10399119692811795799)
XLA Ops:
  1.5 14.0 %all-to-all-start.3 = ((s32[64,1,1]{2,1,0:T(1,128)}), s32[64,1,1]{2,1,0:T(1,128)S(1)}, u32[]{:S(2)}, u32[]{:S(2)}) async-start(s32[64,1,1]{2,1,0:T(1,128)} %copy.65), calls=%async_computation.3 | async-start | bytes 65536 | tf_op jit(solution)/shard_map/all_to_all | solution.py:67
  16.1 6.9 %all-to-all-done.3 = s32[64,1,1]{2,1,0:T(1,128)S(1)} async-done(((s32[64,1,1]{2,1,0:T(1,128)}), s32[64,1,1]{2,1,0:T(1,128)S(1)}, u32[]{:S(2)}, u32[]{:S(2)}) %all-to-all-start.3) | async-done | bytes 288 | tf_op jit(solution)/shard_map/all_to_all | solution.py:67
  23.1 7.1 %all-to-all-start = ((bf16[16,8,128]{2,0,1:T(8,128)(2,1)}), bf16[16,8,128]{2,0,1:T(8,128)(2,1)S(1)}, u32[]{:S(2)}, u32[]{:S(2)}) async-start(bf16[16,8,128]{2,0,1:T(8,128)(2,1)} %copy_bitcast_fusion.2), calls=%async_computation | async-start | bytes 65536 | tf_op jit(solution)/shard_map/all_to_all | solution.py:18
  30.2 1.4 copy_bitcast_fusion.1
  31.5 6.7 %all-to-all-done = bf16[16,8,128]{2,0,1:T(8,128)(2,1)S(1)} async-done(((bf16[16,8,128]{2,0,1:T(8,128)(2,1)}), bf16[16,8,128]{2,0,1:T(8,128)(2,1)S(1)}, u32[]{:S(2)}, u32[]{:S(2)}) %all-to-all-start) | async-done | bytes 32800 | tf_op jit(solution)/shard_map/all_to_all | solution.py:18
  38.2 3.3 %all-to-all-start.2 = ((bf16[16,8,128]{2,0,1:T(8,128)(2,1)}), bf16[16,8,128]{2,0,1:T(8,128)(2,1)S(1)}, u32[]{:S(2)}, u32[]{:S(2)}) async-start(bf16[16,8,128]{2,0,1:T(8,128)(2,1)} %copy_bitcast_fusion.1), calls=%async_computation.2 | async-start | bytes 65536 | tf_op jit(solution)/shard_map/all_to_all | solution.py:19
  41.5 1.8 copy.88
  43.3 6.2 %all-to-all-done.2 = bf16[16,8,128]{2,0,1:T(8,128)(2,1)S(1)} async-done(((bf16[16,8,128]{2,0,1:T(8,128)(2,1)}), bf16[16,8,128]{2,0,1:T(8,128)(2,1)S(1)}, u32[]{:S(2)}, u32[]{:S(2)}) %all-to-all-start.2) | async-done | bytes 32800 | tf_op jit(solution)/shard_map/all_to_all | solution.py:19
  49.5 3.5 %all-to-all-start.1 = ((bf16[16,8,1536]{2,0,1:T(8,128)(2,1)}), bf16[16,8,1536]{2,0,1:T(8,128)(2,1)S(1)}, u32[]{:S(2)}, u32[]{:S(2)}) async-start(bf16[16,8,1536]{2,0,1:T(8,128)(2,1)} %bitcast.129), calls=%async_computation.1 | async-start | bytes 786432 | tf_op jit(solution)/shard_map/all_to_all | solution.py:17
  52.9 1.2 compare_reduce_fusion
  54.2 2.3 broadcast_select_fusion
  56.5 8.8 %all-to-all-done.1 = bf16[16,8,1536]{2,0,1:T(8,128)(2,1)S(1)} async-done(((bf16[16,8,1536]{2,0,1:T(8,128)(2,1)}), bf16[16,8,1536]{2,0,1:T(8,128)(2,1)S(1)}, u32[]{:S(2)}, u32[]{:S(2)}) %all-to-all-start.1) | async-done | bytes 393248 | tf_op jit(solution)/shard_map/all_to_all | solution.py:17
  65.3 7.5 %all-to-all-start.4 = ((bf16[64,128,256]{2,1,0:T(8,128)(2,1)}), bf16[64,128,256]{2,1,0:T(8,128)(2,1)}, u32[]{:S(2)}, u32[]{:S(2)}) async-start(bf16[64,128,256]{2,1,0:T(8,128)(2,1)} %broadcast_select_fusion), calls=%async_computation.4 | async-start | bytes 8388608 | tf_op jit(solution)/shard_map/all_to_all | solution.py:69
  76.9 89.8 %all-to-all-done.4 = bf16[64,128,256]{2,1,0:T(8,128)(2,1)} async-done(((bf16[64,128,256]{2,1,0:T(8,128)(2,1)}), bf16[64,128,256]{2,1,0:T(8,128)(2,1)}, u32[]{:S(2)}, u32[]{:S(2)}) %all-to-all-start.4) | async-done | bytes 4194336 | tf_op jit(solution)/shard_map/all_to_all | solution.py:69
  166.6 4.8 %gather_fusion = bf16[52,128,256]{2,1,0:T(8,128)(2,1)} fusion(bf16[64,128,256]{2,1,0:T(8,128)(2,1)} %all-to-all-done.4, s32[1024]{0:T(1024)S(1)} %pad_clamp_fusion), kind=kCustom, calls=%fused_computation | custom fusion | bytes 6815952 | tf_op jit(solution)/shard_map/jit(_take)/gather | solution.py:71
  171.4 4.8 %bitcast_select_fusion.1 = bf16[26,256,256]{2,1,0:T(8,128)(2,1)} fusion(pred[26,256]{1,0:T(8,128)(4,1)S(1)} %bitcast.171, bf16[26,256,256]{2,1,0:T(8,128)(2,1)} %bitcast.155), kind=kLoop, calls=%fused_computation.20 | loop fusion | flops 1703936 | bytes 6822400 | tf_op jit(solution)/shard_map/jit(_take)/select_n | solution.py:71
  176.2 57.1 %while.16 = (s32[]{:T(128)}, f32[1,12,128]{2,1,0:T(8,128)S(1)}, f32[1,12,128]{2,1,0:T(8,128)S(1)}, f32[128,1,12,128]{0,3,2,1:T(8,128)S(1)}, pred[26,256]{1,0:T(8...) while((s32[]{:T(128)}, f32[1,12,128]{2,1,0:T(8,128)S(1)}, ...), condition=%wide.region_7.8_spmd, body=%wide.region_4.7_spmd.sunk | while | flops 205263360 | bytes 7181405 | solution.py:90
  178.4 0.9 dynamic-slice_bitcast_fusion.2
  180.6 0.9 dynamic-slice_bitcast_fusion.2
  182.8 0.9 dynamic-slice_bitcast_fusion.2
  185.0 0.9 dynamic-slice_bitcast_fusion.2
  187.2 0.9 dynamic-slice_bitcast_fusion.2
  189.4 0.9 dynamic-slice_bitcast_fusion.2
  196.0 0.9 dynamic-slice_bitcast_fusion.2
  198.2 0.9 dynamic-slice_bitcast_fusion.2
  204.8 0.9 dynamic-slice_bitcast_fusion.2
  213.6 0.9 dynamic-slice_bitcast_fusion.2
  220.2 0.9 dynamic-slice_bitcast_fusion.2
  222.4 0.9 dynamic-slice_bitcast_fusion.2
  229.0 0.9 dynamic-slice_bitcast_fusion.2
  231.2 0.9 dynamic-slice_bitcast_fusion.2
  234.1 16.7 %all_to_all.78 = bf16[8,16,1536]{2,1,0:T(8,128)(2,1)S(1)} all-to-all(bf16[8,16,1536]{2,1,0:T(8,128)(2,1)S(1)} %all_to_all.68), channel_id=1, replica_groups=mesh['seq'=64,'tensor'=8] {'tensor'}, dimensions={0} | all-to-all | bytes 786432 | tf_op jit(solution)/shard_map/all_to_all | solution.py:94
  (240 shorter events, 50.2 us)
Async XLA Ops:
  0.0 15.5 %copy-start = (bf16[16,1024]{1,0:T(8,128)(2,1)S(1)}, bf16[16,1024]{1,0:T(8,128)(2,1)}, u32[]{:S(2)}) copy-start(bf16[16,1024]{1,0:T(8,128)(2,1)} %param.12) | copy-start | bytes 98308
  1.5 21.6 %all-to-all-start.3 = ((s32[64,1,1]{2,1,0:T(1,128)}), s32[64,1,1]{2,1,0:T(1,128)S(1)}, u32[]{:S(2)}, u32[]{:S(2)}) async-start(s32[64,1,1]{2,1,0:T(1,128)} %copy.65), calls=%async_computation.3 | async-start | bytes 65536 | tf_op jit(solution)/shard_map/all_to_all | solution.py:67
  23.1 15.1 %all-to-all-start = ((bf16[16,8,128]{2,0,1:T(8,128)(2,1)}), bf16[16,8,128]{2,0,1:T(8,128)(2,1)S(1)}, u32[]{:S(2)}, u32[]{:S(2)}) async-start(bf16[16,8,128]{2,0,1:T(8,128)(2,1)} %copy_bitcast_fusion.2), calls=%async_computation | async-start | bytes 65536 | tf_op jit(solution)/shard_map/all_to_all | solution.py:18
  38.2 11.3 %all-to-all-start.2 = ((bf16[16,8,128]{2,0,1:T(8,128)(2,1)}), bf16[16,8,128]{2,0,1:T(8,128)(2,1)S(1)}, u32[]{:S(2)}, u32[]{:S(2)}) async-start(bf16[16,8,128]{2,0,1:T(8,128)(2,1)} %copy_bitcast_fusion.1), calls=%async_computation.2 | async-start | bytes 65536 | tf_op jit(solution)/shard_map/all_to_all | solution.py:19
  49.5 15.8 %all-to-all-start.1 = ((bf16[16,8,1536]{2,0,1:T(8,128)(2,1)}), bf16[16,8,1536]{2,0,1:T(8,128)(2,1)S(1)}, u32[]{:S(2)}, u32[]{:S(2)}) async-start(bf16[16,8,1536]{2,0,1:T(8,128)(2,1)} %bitcast.129), calls=%async_computation.1 | async-start | bytes 786432 | tf_op jit(solution)/shard_map/all_to_all | solution.py:17
  56.5 16.3 %copy-start.2 = (s32[1,52]{1,0:T(1,128)S(1)}, s32[1,52]{1,0:T(1,128)}, u32[]{:S(2)}) copy-start(s32[1,52]{1,0:T(1,128)} %param.15) | copy-start | bytes 628
  56.5 16.6 %copy-start.1 = (s32[64]{0:T(128)S(1)}, s32[64]{0:T(128)}, u32[]{:S(2)}) copy-start(s32[64]{0:T(128)} %param.14) | copy-start | bytes 772
  65.3 101.3 %all-to-all-start.4 = ((bf16[64,128,256]{2,1,0:T(8,128)(2,1)}), bf16[64,128,256]{2,1,0:T(8,128)(2,1)}, u32[]{:S(2)}, u32[]{:S(2)}) async-start(bf16[64,128,256]{2,1,0:T(8,128)(2,1)} %broadcast_select_fusion), calls=%async_computation.4 | async-start | bytes 8388608 | tf_op jit(solution)/shard_map/all_to_all | solution.py:69
where the time goes:
time: 256 us; the launch traced here: 252 us
  waiting for transfers between devices  118 us (46%)
  local copies, waits for them, and re-layouts  37.6 us (15%)
  starting transfers between devices  35.4 us (14%)
  matrix products  25.1 us (10%)
  blocking collectives  16.7 us (7%)
  other arithmetic  16.6 us (6%)
    all_to_all x1, waiting for transfers between devices, local(): lax.all_to_all(outgoing, 'seq', split_axis=0, concat_axis=0, tiled=True)  89.8 us
    squeeze x26, local copies, waits for them, and re-layouts, local(): lax.scan(step_pair, carry_state, (paired, paired_mask))  23.8 us
    all_to_all x1, blocking collectives, local(): lax.all_to_all(result, 'tensor', split_axis=0, concat_axis=1, tiled=True)  16.7 us
    dot_general x27, matrix products, attend(): jnp.einsum('grik,kgd->igrd', weights, val_block, preferred_element_type=j...  15 us
    all_to_all x1, starting transfers between devices, local(): lax.all_to_all(wanted, 'seq', split_axis=0, concat_axis=0, tiled=True)  14 us
    dot_general x27, matrix products, attend(): jnp.einsum('igrd,kgd->grik', query_four, key_block, preferred_element_typ...  10.1 us
    all_to_all x1, waiting for transfers between devices, local(): lax.all_to_all(queries, 'tensor', split_axis=1, concat_axis=0, tiled=True)  8.77 us
    all_to_all x1, starting transfers between devices, local(): lax.all_to_all(outgoing, 'seq', split_axis=0, concat_axis=0, tiled=True)  7.5 us
  transfers between devices with their start and end apart: 5, of which 5 were waited for; matrix products, arithmetic and copies ran while one was open for 4% of the time, Pallas kernels for 0%

commit v1 on v0

v1 whole, which is shorter than its diff:
```python
import functools
import math

import jax
import jax.numpy as jnp
from jax import lax
from jax.experimental import pallas as pl
from jax.experimental.pallas import tpu as pltpu
from jax.sharding import Mesh, PartitionSpec as P

HEADS = 96
KV = 8
HD = 128
TILE = 128
GROUP = HEADS // KV
NX, NZ, NC, NT = 4, 8, 2, 8
BIG = -1e30
LOG2E = 1.4426950408889634
SCALE2 = LOG2E / math.sqrt(HD)
F32 = jnp.float32
BF16 = jnp.bfloat16


def attend(h, s, vext, m_ref, acc_ref):
    old = m_ref[h]
    top = jnp.max(s, axis=1, keepdims=True)
    new = jnp.maximum(old, top)
    p = jnp.exp2((s - new[:, :1]) * SCALE2).astype(BF16)
    keep = jnp.exp2((old - new) * SCALE2)
    part = jnp.dot(p, vext, preferred_element_type=F32)
    acc_ref[h] = acc_ref[h] * jnp.concatenate([keep, keep], axis=1) + part
    m_ref[h] = new


def query(q_ref, h):
    lane = lax.broadcasted_iota(jnp.int32, (TILE, TILE), 1)
    one = jnp.where(lane == 0, 1.0, 0.0).astype(BF16)
    return jnp.concatenate([q_ref[:, pl.ds(pl.multiple_of(h * HD, HD), HD)], one], axis=1)


def own_tile(own_len, q_ref, own_ref, m_ref, acc_ref):
    row = lax.broadcasted_iota(jnp.int32, (TILE, TILE), 0)
    col = lax.broadcasted_iota(jnp.int32, (TILE, TILE), 1)
    seen = (col <= row) & (col < own_len)
    key = own_ref[:, :HD]
    vext = jnp.concatenate([own_ref[:, HD:], jnp.ones((TILE, HD), BF16)], axis=1)

    def head(h, carry):
        q = q_ref[:, pl.ds(pl.multiple_of(h * HD, HD), HD)]
        s = lax.dot_general(q, key, (((1,), (1,)), ((), ())), preferred_element_type=F32)
        s = jnp.where(seen, s, BIG)
        top = jnp.max(s, axis=1, keepdims=True)
        p = jnp.exp2((s - top) * SCALE2).astype(BF16)
        acc_ref[h] = jnp.dot(p, vext, preferred_element_type=F32)
        m_ref[h] = jnp.broadcast_to(top, (TILE, HD))
        return carry

    lax.fori_loop(0, GROUP, head, 0)


def far_tiles(eff_ref, base, q_ref, kv_ref, key_t, vext, m_ref, acc_ref):
    tiles = kv_ref.shape[0]
    lane = lax.broadcasted_iota(jnp.int32, (TILE, TILE), 1)
    total = eff_ref[base]
    for i in range(1, tiles):
        total = total + eff_ref[base + i]

    @pl.when(total > 0)
    def _():
        for i in range(tiles):
            at = slice(i * TILE, (i + 1) * TILE)
            key_t[:HD, at] = kv_ref[i, :, :HD].T
            key_t[HD:, at] = jnp.where(lane < eff_ref[base + i], 0.0, BIG).astype(BF16)
            vext[at, :HD] = kv_ref[i, :, HD:]
            vext[at, HD:] = jnp.ones((TILE, HD), BF16)

        def head(h, carry):
            s = jnp.dot(query(q_ref, h), key_t[...], preferred_element_type=F32)
            attend(h, s, vext[...], m_ref, acc_ref)
            return carry

        lax.fori_loop(0, GROUP, head, 0)


def first_kernel(eff, q, own, a, b, m, acc, key_t, vext):
    own_tile(eff[0], q, own, m, acc)
    far_tiles(eff, 1, q, a, key_t, vext, m, acc)
    far_tiles(eff, 9, q, b, key_t, vext, m, acc)


def middle_kernel(eff, q, a, b, m_in, acc_in, m, acc, key_t, vext):
    m[...] = m_in[...]
    acc[...] = acc_in[...]
    far_tiles(eff, 0, q, a, key_t, vext, m, acc)
    far_tiles(eff, 8, q, b, key_t, vext, m, acc)


def last_kernel(eff, q, a, b, m_in, acc_in, out, m, acc, key_t, vext):
    m[...] = m_in[...]
    acc[...] = acc_in[...]
    far_tiles(eff, 0, q, a, key_t, vext, m, acc)
    far_tiles(eff, 8, q, b, key_t, vext, m, acc)

    def head(h, carry):
        val = acc[h]
        res = (val[:, :HD] / val[:, HD:]).astype(BF16)
        out[:, pl.ds(pl.multiple_of(h * HD, HD), HD)] = res
        return carry

    lax.fori_loop(0, GROUP, head, 0)


VM = pl.BlockSpec(memory_space=pltpu.VMEM)
SM = pl.BlockSpec(memory_space=pltpu.SMEM)
STATE = (
    jax.ShapeDtypeStruct((GROUP, TILE, HD), F32),
    jax.ShapeDtypeStruct((GROUP, TILE, 2 * HD), F32),
)
WORK = [pltpu.VMEM((2 * HD, NZ * TILE), BF16), pltpu.VMEM((NZ * TILE, 2 * HD), BF16)]
PARAMS = pltpu.CompilerParams(vmem_limit_bytes=24 * 1024 * 1024)


def cost(tiles):
    return pl.CostEstimate(
        flops=tiles * GROUP * TILE * TILE * 256 * 4,
        bytes_accessed=4 * 1024 * 1024,
        transcendentals=tiles * GROUP * TILE * TILE,
    )


def first(eff, q, own, a, b):
    return pl.pallas_call(
        first_kernel,
        out_shape=STATE,
        in_specs=[SM, VM, VM, VM, VM],
        out_specs=(VM, VM),
        scratch_shapes=WORK,
        compiler_params=PARAMS,
        cost_estimate=cost(17),
    )(eff, q, own, a, b)


def middle(eff, q, a, b, state):
    return pl.pallas_call(
        middle_kernel,
        out_shape=STATE,
        in_specs=[SM, VM, VM, VM, VM, VM],
        out_specs=(VM, VM),
        scratch_shapes=WORK,
        compiler_params=PARAMS,
        cost_estimate=cost(16),
    )(eff, q, a, b, *state)


def last(eff, q, a, b, state):
    return pl.pallas_call(
        last_kernel,
        out_shape=jax.ShapeDtypeStruct((TILE, GROUP * HD), BF16),
        in_specs=[SM, VM, VM, VM, VM, VM],
        out_specs=VM,
        scratch_shapes=[pltpu.VMEM(s.shape, s.dtype) for s in STATE] + WORK,
        compiler_params=PARAMS,
        cost_estimate=cost(16),
    )(eff, q, a, b, *state)


def flip(a):
    return lax.ppermute(a, "c", [(0, 1), (1, 0)])


def along(a):
    pairs = []
    for x in range(NX):
        for c in range(NC):
            to = (x + 1) % NX if c == 0 else (x - 1) % NX
            pairs.append((x * NC + c, to * NC + c))
    return lax.ppermute(a, ("x", "c"), pairs)


def local(queries, keys, values, tile_len, ancestors):
    rows = queries.shape[0]
    x, z, c = (lax.axis_index(n) for n in ("x", "z", "c"))

    kv = jnp.concatenate([keys.reshape(rows, KV, HD), values.reshape(rows, KV, HD)], axis=2)
    own = lax.all_to_all(kv.transpose(1, 0, 2), "t", 0, 0, tiled=True).reshape(TILE, 2 * HD)
    line = lax.all_to_all(jnp.broadcast_to(own, (NZ, TILE, 2 * HD)), "z", 0, 0, tiled=True)

    listed = ancestors[0]
    tiles = jnp.arange(tile_len.shape[0], dtype=jnp.int32)
    hit = jnp.any(listed[:, None] == tiles[None, :], axis=0)
    eff = jnp.where(hit, tile_len, 0).reshape(NX, NZ, NC)
    near = jnp.where(c == 0, (x + 3) % NX, (x + 1) % NX)
    other = jnp.where(c == 0, (x + 1) % NX, (x + 3) % NX)
    opposite = (x + 2) % NX

    def lens(xi, ci):
        return lax.dynamic_slice(eff, (xi, 0, ci), (1, NZ, 1)).reshape(NZ)

    own_len = lax.dynamic_slice(tile_len, ((x * NZ + z) * NC + c,), (1,))
    eff0 = jnp.concatenate([own_len, lens(x, c), lens(x, 1 - c)])
    eff1 = jnp.concatenate([lens(near, c), lens(other, 1 - c)])
    eff2 = jnp.concatenate([lens(near, 1 - c), lens(other, c)])
    eff3 = jnp.concatenate([lens(opposite, c), lens(opposite, 1 - c)])

    q = queries.reshape(rows, KV, GROUP * HD).transpose(1, 0, 2)
    q = lax.all_to_all(q, "t", 0, 0, tiled=True).reshape(TILE, GROUP * HD)

    p1 = along(line)
    c0 = flip(line)
    p2 = along(c0)
    state = first(eff0, q, own, line, c0)
    p3 = along(p1)
    c1 = flip(p1)
    state = middle(eff1, q, p1, c1, state)
    c2 = flip(p2)
    state = middle(eff2, q, p2, c2, state)
    c3 = flip(p3)
    out = last(eff3, q, p3, c3, state)

    out = lax.all_to_all(out.reshape(NT, rows, GROUP * HD), "t", 0, 0, tiled=True)
    return out.transpose(1, 0, 2).reshape(rows, HEADS * HD)


def solution(mesh):
    fine = Mesh(mesh.devices.reshape(NX, NZ, NC, NT), ("x", "z", "c", "t"))
    split = P(("x", "z", "c", "t"), None)
    in_specs = (split, split, split, P(), P(("x", "z", "c"), None))
    return jax.shard_map(local, mesh=fine, in_specs=in_specs, out_specs=split, check_vma=False)
```

time: 256 us -> 169 us (0.66)
  the two profiles are of different devices: /device:TPU:6 before, /device:TPU:70 now
where the time goes in v1:
time: 169 us
  Pallas kernels  68.2 us (40%)
  blocking collectives  61.4 us (36%)
  starting transfers between devices  29.5 us (17%)
  local copies, waits for them, and re-layouts  4.17 us (2%)
  waiting for transfers between devices  3.88 us (2%)
    pallas_call x2, Pallas kernels, middle(): pl.pallas_call(middle_kernel, out_shape=STATE, in_specs=[SM, VM, VM, VM,...  36.6 us
    all_to_all x1, blocking collectives, local(): lax.all_to_all(jnp.broadcast_to(own, (NZ, TILE, 2 * HD)), 'z', 0, 0, tile...  24.4 us
    all_to_all x1, blocking collectives, local(): lax.all_to_all(out.reshape(NT, rows, GROUP * HD), 't', 0, 0, tiled=True)  21.8 us
    pallas_call x1, Pallas kernels, last(): pl.pallas_call(last_kernel, out_shape=jax.ShapeDtypeStruct((TILE, GROUP *...  18 us
    ppermute x4, starting transfers between devices, flip(): return lax.ppermute(a, 'c', [(0, 1), (1, 0)])  17.2 us
    all_to_all x1, blocking collectives, local(): lax.all_to_all(kv.transpose(1, 0, 2), 't', 0, 0, tiled=True)  15.3 us
    pallas_call x1, Pallas kernels, first(): pl.pallas_call(first_kernel, out_shape=STATE, in_specs=[SM, VM, VM, VM, V...  13.7 us
    ppermute x3, starting transfers between devices, along(): return lax.ppermute(a, ('x', 'c'), pairs)  8.84 us
  transfers between devices with their start and end apart: 8, of which 1 were waited for; matrix products, arithmetic and copies ran while one was open for 2% of the time, Pallas kernels for 30%

profile of v1, /device:TPU:70, one launch (start us, length us, event | category | flops | bytes accessed | tf_op | source)
XLA Modules:
  0.0 168.6 jit_solution(11706656805236698945)
XLA Ops:
  0.0 0.8 copy-done
  0.8 0.8 copy_bitcast_fusion
  1.6 15.3 %all_to_all.20 = bf16[8,16,256]{2,1,0:T(8,128)(2,1)S(1)} all-to-all(bf16[8,16,256]{2,1,0:T(8,128)(2,1)S(1)} %maximum_bitcast_fusion), channel_id=1, replica_groups=mesh['x'=4,'z'=8,'c'=2,'t'=8] {'t'}, dimensions={0} | all-to-all | bytes 131072 | tf_op jit(solution)/shard_map/all_to_all | solution.py:185
  16.9 24.4 %all_to_all.21.a = bf16[8,128,256]{2,1,0:T(8,128)(2,1)S(1)} all-to-all(bf16[8,128,256]{2,1,0:T(8,128)(2,1)S(1)} %broadcast_in_dim.9), channel_id=1, replica_groups=mesh['x'=4,'z'=8,'c'=2,'t'=8] {'z'}, dimensions={0} | all-to-all | bytes 1048576 | tf_op jit(solution)/shard_map/all_to_all | solution.py:186
  41.3 1.9 %collective-permute-start.3 = (bf16[8,128,256]{2,1,0:T(8,128)(2,1)S(1)}, bf16[8,128,256]{2,1,0:T(8,128)(2,1)S(1)}, u32[]{:S(2)}, u32[]{:S(2)}) collective-permute-start(bf16[8,128,256]{2,1,0:T(8,128)(2,1)S(1)} %all_to_all.21.a), channel_id=1, source_target_pairs={{0,8},{8,0},{1,9},{9,1},{2,10},{10,2},{3,11},{11,3},{4,12},{12,4},... | collective-permute-start | bytes 1572872 | tf_op jit(solution)/shard_map/ppermute | solution.py:168
  43.2 0.8 copy.25
  44.0 3.5 %all-to-all-start = ((bf16[8,16,1536]{2,1,0:T(8,128)(2,1)}), bf16[8,16,1536]{2,1,0:T(8,128)(2,1)S(1)}, u32[]{:S(2)}, u32[]{:S(2)}) async-start(bf16[8,16,1536]{2,1,0:T(8,128)(2,1)} %bitcast.25), calls=%async_computation | async-start | bytes 786432 | tf_op jit(solution)/shard_map/all_to_all | solution.py:206
  47.4 2.4 %collective-permute-start = (bf16[8,128,256]{2,1,0:T(8,128)(2,1)S(1)}, bf16[8,128,256]{2,1,0:T(8,128)(2,1)S(1)}, u32[]{:S(2)}, u32[]{:S(2)}) collective-permute-start(bf16[8,128,256]{2,1,0:T(8,128)(2,1)S(1)} %all_to_all.21.a), channel_id=1, source_target_pairs={{0,128},{8,392},{128,256},{136,8},{256,384},{264,136},{384,0},{392... | collective-permute-start | bytes 1572872 | tf_op jit(solution)/shard_map/ppermute | solution.py:177
  49.8 0.1 fusion
  49.9 0.0 collective-permute-done.3.b
  49.9 3.4 %collective-permute-start.4 = (bf16[8,128,256]{2,1,0:T(8,128)(2,1)S(1)}, bf16[8,128,256]{2,1,0:T(8,128)(2,1)S(1)}, u32[]{:S(2)}, u32[]{:S(2)}) collective-permute-start(bf16[8,128,256]{2,1,0:T(8,128)(2,1)S(1)} %collective-permute-done.3.b), channel_id=1, source_target_pairs={{0,128},{8,392},{128,256},{136,8},{256,384},{264,136},{384,0},{392... | collective-permute-start | bytes 1572872 | tf_op jit(solution)/shard_map/ppermute | solution.py:177
  53.4 0.1 reshape.49
  53.5 0.7 dynamic_slice.33
  54.2 0.3 dynamic-slice_reduce_fusion.1
  54.5 0.1 pad_add_fusion.2.eff
  54.5 0.1 pad_add_fusion.1.eff
  54.6 3.9 %collective-permute-done.a = bf16[8,128,256]{2,1,0:T(8,128)(2,1)S(1)} collective-permute-done((bf16[8,128,256]{2,1,0:T(8,128)(2,1)S(1)}, bf16[8,128,256]{2,1,0:T(8,128)(2,1)S(1)}, u32[]{:S(2)}, u32[]{:S(2)}) %collective-permute-start) | collective-permute-done | bytes 524320 | tf_op jit(solution)/shard_map/ppermute | solution.py:177
  58.5 2.5 %collective-permute-start.6 = (bf16[8,128,256]{2,1,0:T(8,128)(2,1)S(1)}, bf16[8,128,256]{2,1,0:T(8,128)(2,1)}, u32[]{:S(2)}, u32[]{:S(2)}) collective-permute-start(bf16[8,128,256]{2,1,0:T(8,128)(2,1)S(1)} %collective-permute-done.a), channel_id=1, source_target_pairs={{0,8},{8,0},{1,9},{9,1},{2,10},{10,2},{3,11},{11,3},{4,12},{12,4},... | collective-permute-start | bytes 1572872 | tf_op jit(solution)/shard_map/ppermute | solution.py:168
  61.0 3.0 %collective-permute-start.1 = (bf16[8,128,256]{2,1,0:T(8,128)(2,1)S(1)}, bf16[8,128,256]{2,1,0:T(8,128)(2,1)S(1)}, u32[]{:S(2)}, u32[]{:S(2)}) collective-permute-start(bf16[8,128,256]{2,1,0:T(8,128)(2,1)S(1)} %collective-permute-done.a), channel_id=1, source_target_pairs={{0,128},{8,392},{128,256},{136,8},{256,384},{264,136},{384,0},{392... | collective-permute-start | bytes 1572872 | tf_op jit(solution)/shard_map/ppermute | solution.py:177
  64.0 0.1 pad_add_fusion.eff
  64.1 0.8 pad_add_fusion.3.eff
  64.9 1.9 %collective-permute-start.5 = (bf16[8,128,256]{2,1,0:T(8,128)(2,1)S(1)}, bf16[8,128,256]{2,1,0:T(8,128)(2,1)}, u32[]{:S(2)}, u32[]{:S(2)}) collective-permute-start(bf16[8,128,256]{2,1,0:T(8,128)(2,1)S(1)} %collective-permute-done.4.a), channel_id=1, source_target_pairs={{0,8},{8,0},{1,9},{9,1},{2,10},{10,2},{3,11},{11,3},{4,12},{12,4},... | collective-permute-start | bytes 1572872 | tf_op jit(solution)/shard_map/ppermute | solution.py:168
  66.8 13.7 %shard_map.55 = (f32[12,128,128]{2,1,0:T(8,128)S(1)}, f32[12,128,256]{2,1,0:T(8,128)S(1)}) custom-call(s32[17]{0:T(128)S(1)} %pad_add_fusion.3.eff, bf16[128,1536]{1,0:T(8,128)(2,1)S(1)} %bitcast.26, bf16[128,256]{1,0:T(8,128)(2,1)S(1)} %bitcast.32, bf16[8,128,256]{2,1,0:T(8,128)(2,1)S(1)} %all_to_all.21.a, bf16[8,128,256]{2,1,0:T(8,128)(2,1)S(1)} %collective-permute-done.3.b), custom_call_target="tpu_custom_call" | custom-call | flops 3422552064 | bytes 4194304 | tf_op jit(solution)/shard_map/pallas_call | solution.py:132
  80.5 0.0 collective-permute-done.1.a
  80.5 10.9 %collective-permute-start.2 = (bf16[8,128,256]{2,1,0:T(8,128)(2,1)S(1)}, bf16[8,128,256]{2,1,0:T(8,128)(2,1)S(1)}, u32[]{:S(2)}, u32[]{:S(2)}) collective-permute-start(bf16[8,128,256]{2,1,0:T(8,128)(2,1)S(1)} %collective-permute-done.1.a), channel_id=1, source_target_pairs={{0,8},{8,0},{1,9},{9,1},{2,10},{10,2},{3,11},{11,3},{4,12},{12,4},... | collective-permute-start | bytes 1572872 | tf_op jit(solution)/shard_map/ppermute | solution.py:168
  91.4 0.0 collective-permute-done.6.b
  91.5 18.3 %shard_map.56 = (f32[12,128,128]{2,1,0:T(8,128)S(1)}, f32[12,128,256]{2,1,0:T(8,128)S(1)}) custom-call(s32[16]{0:T(128)S(1)} %pad_add_fusion.2.eff, bf16[128,1536]{1,0:T(8,128)(2,1)S(1)} %bitcast.27, bf16[8,128,256]{2,1,0:T(8,128)(2,1)S(1)} %collective-permute-done.a, bf16[8,128,256]{2,1,0:T(8,128)(2,1)} %collective-permute-done.6.b, ...), custom_call_target="tpu_custom_call" | custom-call | flops 3221225472 | bytes 4194304 | tf_op jit(solution)/shard_map/pallas_call | solution.py:144
  109.7 0.0 collective-permute-done.5.b
  109.7 18.3 %shard_map.57 = (f32[12,128,128]{2,1,0:T(8,128)S(1)}, f32[12,128,256]{2,1,0:T(8,128)S(1)}) custom-call(s32[16]{0:T(128)S(1)} %pad_add_fusion.1.eff, bf16[128,1536]{1,0:T(8,128)(2,1)S(1)} %bitcast.28, bf16[8,128,256]{2,1,0:T(8,128)(2,1)S(1)} %collective-permute-done.4.a, bf16[8,128,256]{2,1,0:T(8,128)(2,1)} %collective-permute-done.5.b, ...), custom_call_target="tpu_custom_call" | custom-call | flops 3221225472 | bytes 4194304 | tf_op jit(solution)/shard_map/pallas_call | solution.py:144
  128.1 18.0 %shard_map.58 = bf16[128,1536]{1,0:T(8,128)(2,1)S(1)} custom-call(s32[16]{0:T(128)S(1)} %pad_add_fusion.eff, bf16[128,1536]{1,0:T(8,128)(2,1)S(1)} %bitcast.29, bf16[8,128,256]{2,1,0:T(8,128)(2,1)S(1)} %collective-permute-done.1.a, bf16[8,128,256]{2,1,0:T(8,128)(2,1)S(1)} %collective-permute-done.2.b, f32[12,128,128]{2,1,0:T(8,128)S(1)} %get-tuple-element.15.m_in, ...), custom_call_target="tpu_custom_call" | custom-call | flops 3221225472 | bytes 4194304 | tf_op jit(solution)/shard_map/pallas_call | solution.py:156
  146.1 21.8 %all_to_all.22 = bf16[8,16,1536]{2,1,0:T(8,128)(2,1)S(1)} all-to-all(bf16[8,16,1536]{2,1,0:T(8,128)(2,1)S(1)} %bitcast.30), channel_id=1, replica_groups=mesh['x'=4,'z'=8,'c'=2,'t'=8] {'t'}, dimensions={0} | all-to-all | bytes 786432 | tf_op jit(solution)/shard_map/all_to_all | solution.py:220
  167.8 0.8 copy.21
  (13 shorter events, 0.1 us)
Async XLA Ops:
  0.0 0.8 copy-start
  0.0 43.2 %copy-start.1 = (bf16[16,12288]{1,0:T(8,128)(2,1)S(1)}, bf16[16,12288]{1,0:T(8,128)(2,1)}, u32[]{:S(2)}) copy-start(bf16[16,12288]{1,0:T(8,128)(2,1)} %param.5) | copy-start | bytes 1179652
  16.8 33.0 %copy-start.2 = (s32[1,52]{1,0:T(1,128)S(1)}, s32[1,52]{1,0:T(1,128)}, u32[]{:S(2)}) copy-start(s32[1,52]{1,0:T(1,128)} %param.9) | copy-start | bytes 628
  16.8 36.5 %copy-start.3 = (s32[64]{0:T(128)S(1)}, s32[64]{0:T(128)}, u32[]{:S(2)}) copy-start(s32[64]{0:T(128)} %param.8) | copy-start | bytes 772
  41.3 8.7 %collective-permute-start.3 = (bf16[8,128,256]{2,1,0:T(8,128)(2,1)S(1)}, bf16[8,128,256]{2,1,0:T(8,128)(2,1)S(1)}, u32[]{:S(2)}, u32[]{:S(2)}) collective-permute-start(bf16[8,128,256]{2,1,0:T(8,128)(2,1)S(1)} %all_to_all.21.a), channel_id=1, source_target_pairs={{0,8},{8,0},{1,9},{9,1},{2,10},{10,2},{3,11},{11,3},{4,12},{12,4},... | collective-permute-start | bytes 1572872 | tf_op jit(solution)/shard_map/ppermute | solution.py:168
  44.0 22.8 %all-to-all-start = ((bf16[8,16,1536]{2,1,0:T(8,128)(2,1)}), bf16[8,16,1536]{2,1,0:T(8,128)(2,1)S(1)}, u32[]{:S(2)}, u32[]{:S(2)}) async-start(bf16[8,16,1536]{2,1,0:T(8,128)(2,1)} %bitcast.25), calls=%async_computation | async-start | bytes 786432 | tf_op jit(solution)/shard_map/all_to_all | solution.py:206
  47.4 11.1 %collective-permute-start = (bf16[8,128,256]{2,1,0:T(8,128)(2,1)S(1)}, bf16[8,128,256]{2,1,0:T(8,128)(2,1)S(1)}, u32[]{:S(2)}, u32[]{:S(2)}) collective-permute-start(bf16[8,128,256]{2,1,0:T(8,128)(2,1)S(1)} %all_to_all.21.a), channel_id=1, source_target_pairs={{0,128},{8,392},{128,256},{136,8},{256,384},{264,136},{384,0},{392... | collective-permute-start | bytes 1572872 | tf_op jit(solution)/shard_map/ppermute | solution.py:177
  49.9 14.9 %collective-permute-start.4 = (bf16[8,128,256]{2,1,0:T(8,128)(2,1)S(1)}, bf16[8,128,256]{2,1,0:T(8,128)(2,1)S(1)}, u32[]{:S(2)}, u32[]{:S(2)}) collective-permute-start(bf16[8,128,256]{2,1,0:T(8,128)(2,1)S(1)} %collective-permute-done.3.b), channel_id=1, source_target_pairs={{0,128},{8,392},{128,256},{136,8},{256,384},{264,136},{384,0},{392... | collective-permute-start | bytes 1572872 | tf_op jit(solution)/shard_map/ppermute | solution.py:177
  58.5 33.0 %collective-permute-start.6 = (bf16[8,128,256]{2,1,0:T(8,128)(2,1)S(1)}, bf16[8,128,256]{2,1,0:T(8,128)(2,1)}, u32[]{:S(2)}, u32[]{:S(2)}) collective-permute-start(bf16[8,128,256]{2,1,0:T(8,128)(2,1)S(1)} %collective-permute-done.a), channel_id=1, source_target_pairs={{0,8},{8,0},{1,9},{9,1},{2,10},{10,2},{3,11},{11,3},{4,12},{12,4},... | collective-permute-start | bytes 1572872 | tf_op jit(solution)/shard_map/ppermute | solution.py:168
  61.0 19.5 %collective-permute-start.1 = (bf16[8,128,256]{2,1,0:T(8,128)(2,1)S(1)}, bf16[8,128,256]{2,1,0:T(8,128)(2,1)S(1)}, u32[]{:S(2)}, u32[]{:S(2)}) collective-permute-start(bf16[8,128,256]{2,1,0:T(8,128)(2,1)S(1)} %collective-permute-done.a), channel_id=1, source_target_pairs={{0,128},{8,392},{128,256},{136,8},{256,384},{264,136},{384,0},{392... | collective-permute-start | bytes 1572872 | tf_op jit(solution)/shard_map/ppermute | solution.py:177
  64.9 44.9 %collective-permute-start.5 = (bf16[8,128,256]{2,1,0:T(8,128)(2,1)S(1)}, bf16[8,128,256]{2,1,0:T(8,128)(2,1)}, u32[]{:S(2)}, u32[]{:S(2)}) collective-permute-start(bf16[8,128,256]{2,1,0:T(8,128)(2,1)S(1)} %collective-permute-done.4.a), channel_id=1, source_target_pairs={{0,8},{8,0},{1,9},{9,1},{2,10},{10,2},{3,11},{11,3},{4,12},{12,4},... | collective-permute-start | bytes 1572872 | tf_op jit(solution)/shard_map/ppermute | solution.py:168
  80.5 47.6 %collective-permute-start.2 = (bf16[8,128,256]{2,1,0:T(8,128)(2,1)S(1)}, bf16[8,128,256]{2,1,0:T(8,128)(2,1)S(1)}, u32[]{:S(2)}, u32[]{:S(2)}) collective-permute-start(bf16[8,128,256]{2,1,0:T(8,128)(2,1)S(1)} %collective-permute-done.1.a), channel_id=1, source_target_pairs={{0,8},{8,0},{1,9},{9,1},{2,10},{10,2},{3,11},{11,3},{4,12},{12,4},... | collective-permute-start | bytes 1572872 | tf_op jit(solution)/shard_map/ppermute | solution.py:168

commit v2 on v1

v2 whole, which is shorter than its diff:
```python
import functools
import math

import jax
import jax.numpy as jnp
from jax import lax
from jax.experimental import pallas as pl
from jax.experimental.pallas import tpu as pltpu
from jax.sharding import Mesh, PartitionSpec as P

HEADS = 96
KV = 8
HD = 128
TILE = 128
GROUP = HEADS // KV
NX, NZ, NC, NT = 4, 8, 2, 8
BIG = -1e30
STEP = 16
WIDE = 512
LOG2E = 1.4426950408889634
SCALE2 = LOG2E / math.sqrt(HD)
F32 = jnp.float32
BF16 = jnp.bfloat16


def soften(s, old):
    parts = [s[:, j : j + HD] for j in range(0, s.shape[1], HD)]
    top = functools.reduce(jnp.maximum, parts)
    new = jnp.maximum(old, jnp.max(top, axis=1, keepdims=True))
    p = jnp.concatenate([jnp.exp2((x - new) * SCALE2).astype(BF16) for x in parts], axis=1)
    return p, jnp.exp2((old - new) * SCALE2), new


def own_tile(own_len, q_ref, own_ref, m_ref, acc_ref):
    row = lax.broadcasted_iota(jnp.int32, (TILE, TILE), 0)
    col = lax.broadcasted_iota(jnp.int32, (TILE, TILE), 1)
    seen = (col <= row) & (col < own_len)
    key_t = own_ref[:, :HD].T
    vext = jnp.concatenate([own_ref[:, HD:], jnp.ones((TILE, HD), BF16)], axis=1)
    for h in range(GROUP):
        s = jnp.dot(q_ref[:, h * HD : (h + 1) * HD], key_t, preferred_element_type=F32)
        s = jnp.where(seen, s, BIG)
        top = jnp.broadcast_to(jnp.max(s, axis=1, keepdims=True), (TILE, HD))
        p = jnp.exp2((s - top) * SCALE2).astype(BF16)
        acc_ref[h] = jnp.dot(p, vext, preferred_element_type=F32)
        m_ref[h] = top


def far_tiles(eff_ref, base, q_ref, kv_refs, packed, bias, m_ref, acc_ref):
    row = lax.broadcasted_iota(jnp.int32, (TILE, HD), 0)
    lane = lax.broadcasted_iota(jnp.int32, (TILE, HD), 1)
    one = jnp.where(lane == 0, 1.0, 0.0).astype(BF16)
    count = jnp.int32(0)
    slot = base
    for kv_ref in kv_refs:
        for i in range(kv_ref.shape[0]):
            valid = eff_ref[slot]
            at = pl.ds(pl.multiple_of(count, STEP), TILE)
            packed[at, :] = kv_ref[i]
            bias[at, :] = jnp.where(row < valid, 0.0, BIG).astype(BF16)
            count = count + lax.div(valid + (STEP - 1), STEP) * STEP
            slot += 1
    at = pl.ds(pl.multiple_of(count, STEP), WIDE)
    packed[at, :] = jnp.zeros((WIDE, 2 * HD), BF16)
    bias[at, :] = jnp.full((WIDE, HD), BIG, BF16)

    def block(start, size):
        at = pl.ds(pl.multiple_of(start, WIDE // 2), size)
        key_t = jnp.concatenate([packed[at, :HD].T, bias[at, :].T], axis=0)
        vext = jnp.concatenate([packed[at, HD:], jnp.ones((size, HD), BF16)], axis=1)
        for h in range(GROUP):
            q = jnp.concatenate([q_ref[:, h * HD : (h + 1) * HD], one], axis=1)
            s = jnp.dot(q, key_t, preferred_element_type=F32)
            p, keep, m_ref[h] = soften(s, m_ref[h])
            part = jnp.dot(p, vext, preferred_element_type=F32)
            acc_ref[h] = acc_ref[h] * jnp.concatenate([keep, keep], axis=1) + part

    def step(k, carry):
        block(k * WIDE, WIDE)
        return carry

    wide = lax.div(count + (WIDE // 2 - 1), WIDE)
    lax.fori_loop(0, wide, step, 0)

    @pl.when(count > wide * WIDE)
    def _():
        block(wide * WIDE, WIDE // 2)


def first_kernel(base, eff, q, own, a, b, m, acc, packed, bias):
    own_tile(eff[64], q, own, m, acc)
    far_tiles(eff, base, q, (a, b), packed, bias, m, acc)


def middle_kernel(base, eff, q, a, b, m_in, acc_in, m, acc, packed, bias):
    m[...] = m_in[...]
    acc[...] = acc_in[...]
    far_tiles(eff, base, q, (a, b), packed, bias, m, acc)


def last_kernel(base, eff, q, a, b, m_in, acc_in, out, m, acc, packed, bias):
    m[...] = m_in[...]
    acc[...] = acc_in[...]
    far_tiles(eff, base, q, (a, b), packed, bias, m, acc)
    for h in range(GROUP):
        val = acc[h]
        out[:, h * HD : (h + 1) * HD] = (val[:, :HD] / val[:, HD:]).astype(BF16)


VM = pl.BlockSpec(memory_space=pltpu.VMEM)
SM = pl.BlockSpec(memory_space=pltpu.SMEM)
STATE = (
    jax.ShapeDtypeStruct((GROUP, TILE, HD), F32),
    jax.ShapeDtypeStruct((GROUP, TILE, 2 * HD), F32),
)
ROWS = 2 * NZ * TILE + WIDE
WORK = [pltpu.VMEM((ROWS, 2 * HD), BF16), pltpu.VMEM((ROWS, HD), BF16)]
PARAMS = pltpu.CompilerParams(vmem_limit_bytes=24 * 1024 * 1024)


def busy(us):
    return pl.CostEstimate(flops=int(us * 1e9), bytes_accessed=1024, transcendentals=1024)


LIGHT = pl.CostEstimate(flops=1, bytes_accessed=1, transcendentals=1)


def first(base, eff, q, own, a, b):
    return pl.pallas_call(
        functools.partial(first_kernel, base),
        out_shape=STATE,
        in_specs=[SM, VM, VM, VM, VM],
        out_specs=(VM, VM),
        scratch_shapes=WORK,
        compiler_params=PARAMS,
        cost_estimate=busy(6),
    )(eff, q, own, a, b)


def middle(base, eff, q, a, b, state):
    return pl.pallas_call(
        functools.partial(middle_kernel, base),
        out_shape=STATE,
        in_specs=[SM, VM, VM, VM, VM, VM],
        out_specs=(VM, VM),
        scratch_shapes=WORK,
        compiler_params=PARAMS,
        cost_estimate=busy(5),
    )(eff, q, a, b, *state)


def last(base, eff, q, a, b, state):
    return pl.pallas_call(
        functools.partial(last_kernel, base),
        out_shape=jax.ShapeDtypeStruct((TILE, GROUP * HD), BF16),
        in_specs=[SM, VM, VM, VM, VM, VM],
        out_specs=VM,
        scratch_shapes=[pltpu.VMEM(s.shape, s.dtype) for s in STATE] + WORK,
        compiler_params=PARAMS,
        cost_estimate=busy(4),
    )(eff, q, a, b, *state)


def flip(a):
    return lax.ppermute(a, "c", [(0, 1), (1, 0)])


def along(a, step, wanted):
    pairs = []
    for x in range(NX):
        for c in range(NC):
            to = (x + step) % NX if c == 0 else (x - step) % NX
            if (c, x, to) in wanted:
                pairs.append((x * NC + c, to * NC + c))
    return lax.ppermute(a, ("x", "c"), pairs)


def flip_from(a, low):
    pairs = [(x * NC + c, x * NC + 1 - c) for x in range(low, NX) for c in range(NC)]
    return lax.ppermute(a, ("x", "c"), pairs)


NEXT = {(c, x, x + 1) for c in range(NC) for x in range(NX - 1)} | {(c, 0, NX - 1) for c in range(NC)}
FIRST = NEXT | {(1, 1, 0)}
THIRD = {(0, 1, 2), (0, 2, 3), (1, 3, 2), (1, 0, 3)}


barrier = lax.optimization_barrier


def seen_lengths(tile_len, listed, x, z, c):
    i = jnp.arange(72, dtype=jnp.int32)
    buf, slot = i // 8, i % 8
    core = jnp.where(buf % 2 == 0, c, 1 - c)
    side = jnp.where(c == 0, -1, 1)
    dx = jnp.where((buf < 2) | (buf == 8), 0, jnp.where(buf >= 6, 2, jnp.where((buf == 2) | (buf == 5), side, -side)))
    zi = jnp.where(buf == 8, z, slot)
    ids = (((x + dx) % NX) * NZ + zi) * NC + core
    hit = jnp.any(ids[:, None] == listed[None, :], axis=1) | (buf == 8)
    tiles = jnp.arange(tile_len.shape[0], dtype=jnp.int32)
    return jnp.sum(jnp.where((ids[:, None] == tiles[None, :]) & hit[:, None], tile_len[None, :], 0), axis=1)


def spread_kernel(k, v, out):
    for h in range(KV):
        at = slice(h * HD, (h + 1) * HD)
        out[h, :, :HD] = k[:, at]
        out[h, :, HD:] = v[:, at]


def spread(keys, values):
    return pl.pallas_call(
        spread_kernel,
        out_shape=jax.ShapeDtypeStruct((KV, keys.shape[0], 2 * HD), BF16),
        in_specs=[VM, VM],
        out_specs=VM,
        cost_estimate=LIGHT,
    )(keys, values)


def local(queries, keys, values, tile_len, ancestors):
    rows = queries.shape[0]
    x, z, c = (lax.axis_index(n) for n in ("x", "z", "c"))

    own = lax.all_to_all(spread(keys, values), "t", 0, 0, tiled=True).reshape(TILE, 2 * HD)
    line = lax.all_to_all(jnp.broadcast_to(own, (NZ, TILE, 2 * HD)), "z", 0, 0, tiled=True)

    eff = seen_lengths(tile_len, ancestors[0], x, z, c)
    q = queries.reshape(rows, KV, GROUP * HD).transpose(1, 0, 2)
    q, eff, line = barrier((q, eff, line))
    q = lax.all_to_all(q, "t", 0, 0, tiled=True).reshape(TILE, GROUP * HD)

    p1 = along(line, 1, FIRST)
    p2 = along(line, -1, NEXT)
    c0 = flip(line)
    state = first(0, eff, q, own, line, c0)
    p3 = along(p1, 1, THIRD)
    c1 = flip_from(p1, 1)
    state = middle(16, eff, q, p1, c1, state)
    c2 = flip_from(p2, 1)
    c3 = flip_from(p3, 2)
    state = middle(32, eff, q, p2, c2, state)
    out = last(48, eff, q, p3, c3, state)

    out = lax.all_to_all(out.reshape(NT, rows, GROUP * HD), "t", 0, 0, tiled=True)
    return out.transpose(1, 0, 2).reshape(rows, HEADS * HD)


def solution(mesh):
    fine = Mesh(mesh.devices.reshape(NX, NZ, NC, NT), ("x", "z", "c", "t"))
    split = P(("x", "z", "c", "t"), None)
    in_specs = (split, split, split, P(), P(("x", "z", "c"), None))
    return jax.shard_map(local, mesh=fine, in_specs=in_specs, out_specs=split, check_vma=False)
```

time: 169 us -> 113 us (0.67)
  the two profiles are of different devices: /device:TPU:70 before, /device:TPU:6 now
where the time goes in v2:
time: 113 us; the launch traced here: 112 us
  blocking collectives  37 us (33%)
  starting transfers between devices  27.2 us (24%)
  waiting for transfers between devices  25.8 us (23%)
  Pallas kernels  17.4 us (15%)
  local copies, waits for them, and re-layouts  4.21 us (4%)
    all_to_all x1, blocking collectives, local(): lax.all_to_all(out.reshape(NT, rows, GROUP * HD), 't', 0, 0, tiled=True)  21.5 us
    all_to_all x1, blocking collectives, local(): lax.all_to_all(spread(keys, values), 't', 0, 0, tiled=True)  15.5 us
    all_to_all x1, waiting for transfers between devices, local(): lax.all_to_all(jnp.broadcast_to(own, (NZ, TILE, 2 * HD)), 'z', 0, 0, tile...  15.1 us
    ppermute x3, waiting for transfers between devices, along(): return lax.ppermute(a, ('x', 'c'), pairs)  10.8 us
    all_to_all x1, starting transfers between devices, local(): lax.all_to_all(jnp.broadcast_to(own, (NZ, TILE, 2 * HD)), 'z', 0, 0, tile...  10.3 us
    pallas_call x2, Pallas kernels, middle(): pl.pallas_call(functools.partial(middle_kernel, base), out_shape=STATE, i...  8.69 us
    ppermute x3, starting transfers between devices, flip_from(): return lax.ppermute(a, ('x', 'c'), pairs)  7.64 us
    ppermute x3, starting transfers between devices, along(): return lax.ppermute(a, ('x', 'c'), pairs)  3.88 us
  transfers between devices with their start and end apart: 9, of which 3 were waited for; matrix products, arithmetic and copies ran while one was open for 1% of the time, Pallas kernels for 11%

profile of v2, /device:TPU:6, one launch (start us, length us, event | category | flops | bytes accessed | tf_op | source)
XLA Modules:
  0.0 112.0 jit_solution(18303482502351672538)
XLA Ops:
  0.0 1.5 %shard_map.55 = bf16[8,16,256]{2,1,0:T(8,128)(2,1)} custom-call(bf16[16,1024]{1,0:T(8,128)(2,1)} %k.1, bf16[16,1024]{1,0:T(8,128)(2,1)} %v.1), custom_call_target="tpu_custom_call" | custom-call | flops 1 | bytes 1 | tf_op jit(solution)/shard_map/pallas_call | solution.py:212
  1.5 15.5 %all_to_all.20 = bf16[8,16,256]{2,1,0:T(8,128)(2,1)S(1)} all-to-all(bf16[8,16,256]{2,1,0:T(8,128)(2,1)} %shard_map.55), channel_id=1, replica_groups=mesh['x'=4,'z'=8,'c'=2,'t'=8] {'t'}, dimensions={0} | all-to-all | bytes 131072 | tf_op jit(solution)/shard_map/all_to_all | solution.py:225
  16.9 0.8 broadcast_in_dim.50
  17.8 10.3 %all-to-all-start.1 = ((bf16[8,128,256]{2,1,0:T(8,128)(2,1)}), bf16[8,128,256]{2,1,0:T(8,128)(2,1)S(1)}, u32[]{:S(2)}, u32[]{:S(2)}) async-start(bf16[8,128,256]{2,1,0:T(8,128)(2,1)} %broadcast_in_dim.50), calls=%async_computation.1 | async-start | bytes 1048576 | tf_op jit(solution)/shard_map/all_to_all | solution.py:226
  28.1 0.8 copy.13
  28.9 0.1 compare_reduce_fusion
  29.0 0.1 select_reduce_fusion.eff
  29.1 15.1 %all-to-all-done.1.a = bf16[8,128,256]{2,1,0:T(8,128)(2,1)S(1)} async-done(((bf16[8,128,256]{2,1,0:T(8,128)(2,1)}), bf16[8,128,256]{2,1,0:T(8,128)(2,1)S(1)}, u32[]{:S(2)}, u32[]{:S(2)}) %all-to-all-start.1) | async-done | bytes 524320 | tf_op jit(solution)/shard_map/all_to_all | solution.py:226
  44.2 3.5 %all-to-all-start.2 = ((bf16[8,16,1536]{2,1,0:T(8,128)(2,1)}), bf16[8,16,1536]{2,1,0:T(8,128)(2,1)S(1)}, u32[]{:S(2)}, u32[]{:S(2)}) async-start(bf16[8,16,1536]{2,1,0:T(8,128)(2,1)} %bitcast.13), calls=%async_computation.2 | async-start | bytes 786432 | tf_op jit(solution)/shard_map/all_to_all | solution.py:231
  47.6 1.3 %collective-permute-start = (bf16[8,128,256]{2,1,0:T(8,128)(2,1)S(1)}, bf16[8,128,256]{2,1,0:T(8,128)(2,1)S(1)}, u32[]{:S(2)}, u32[]{:S(2)}) collective-permute-start(bf16[8,128,256]{2,1,0:T(8,128)(2,1)S(1)} %all-to-all-done.1.a), channel_id=1, source_target_pairs={{0,128},{8,392},{128,256},{136,8},{256,384},{1,129},{9,393},{129,2... | collective-permute-start | bytes 1572872 | tf_op jit(solution)/shard_map/ppermute | solution.py:175
  48.9 1.3 %collective-permute-start.3 = (bf16[8,128,256]{2,1,0:T(8,128)(2,1)S(1)}, bf16[8,128,256]{2,1,0:T(8,128)(2,1)S(1)}, u32[]{:S(2)}, u32[]{:S(2)}) collective-permute-start(bf16[8,128,256]{2,1,0:T(8,128)(2,1)S(1)} %all-to-all-done.1.a), channel_id=1, source_target_pairs={{0,384},{8,136},{136,264},{264,392},{1,385},{9,137},{137,265},{265... | collective-permute-start | bytes 1572872 | tf_op jit(solution)/shard_map/ppermute | solution.py:175
  50.2 1.9 %collective-permute-start.6 = (bf16[8,128,256]{2,1,0:T(8,128)(2,1)S(1)}, bf16[8,128,256]{2,1,0:T(8,128)(2,1)S(1)}, u32[]{:S(2)}, u32[]{:S(2)}) collective-permute-start(bf16[8,128,256]{2,1,0:T(8,128)(2,1)S(1)} %all-to-all-done.1.a), channel_id=1, source_target_pairs={{0,8},{8,0},{1,9},{9,1},{2,10},{10,2},{3,11},{11,3},{4,12},{12,4},... | collective-permute-start | bytes 1572872 | tf_op jit(solution)/shard_map/ppermute | solution.py:165
  52.2 9.7 %collective-permute-done.a = bf16[8,128,256]{2,1,0:T(8,128)(2,1)S(1)} collective-permute-done((bf16[8,128,256]{2,1,0:T(8,128)(2,1)S(1)}, bf16[8,128,256]{2,1,0:T(8,128)(2,1)S(1)}, u32[]{:S(2)}, u32[]{:S(2)}) %collective-permute-start) | collective-permute-done | bytes 524320 | tf_op jit(solution)/shard_map/ppermute | solution.py:175
  61.8 1.9 %collective-permute-start.5 = (bf16[8,128,256]{2,1,0:T(8,128)(2,1)S(1)}, bf16[8,128,256]{2,1,0:T(8,128)(2,1)S(1)}, u32[]{:S(2)}, u32[]{:S(2)}) collective-permute-start(bf16[8,128,256]{2,1,0:T(8,128)(2,1)S(1)} %collective-permute-done.a), channel_id=1, source_target_pairs={{128,136},{136,128},{256,264},{264,256},{384,392},{392,384},{129,1... | collective-permute-start | bytes 1572872 | tf_op jit(solution)/shard_map/ppermute | solution.py:180
  63.7 1.3 %collective-permute-start.1 = (bf16[8,128,256]{2,1,0:T(8,128)(2,1)S(1)}, bf16[8,128,256]{2,1,0:T(8,128)(2,1)S(1)}, u32[]{:S(2)}, u32[]{:S(2)}) collective-permute-start(bf16[8,128,256]{2,1,0:T(8,128)(2,1)S(1)} %collective-permute-done.a), channel_id=1, source_target_pairs={{8,392},{128,256},{256,384},{392,264},{9,393},{129,257},{257,385},... | collective-permute-start | bytes 1572872 | tf_op jit(solution)/shard_map/ppermute | solution.py:175
  65.0 0.0 collective-permute-done.3.a
  65.1 3.3 %collective-permute-start.4 = (bf16[8,128,256]{2,1,0:T(8,128)(2,1)S(1)}, bf16[8,128,256]{2,1,0:T(8,128)(2,1)}, u32[]{:S(2)}, u32[]{:S(2)}) collective-permute-start(bf16[8,128,256]{2,1,0:T(8,128)(2,1)S(1)} %collective-permute-done.3.a), channel_id=1, source_target_pairs={{128,136},{136,128},{256,264},{264,256},{384,392},{392,384},{129,1... | collective-permute-start | bytes 1572872 | tf_op jit(solution)/shard_map/ppermute | solution.py:180
  68.3 0.0 collective-permute-done.6.b
  68.4 0.8 copy-done
  69.1 0.0 all-to-all-done.2
  69.1 1.0 copy-done.1
  70.2 3.5 %shard_map.56 = (f32[12,128,128]{2,1,0:T(8,128)S(1)}, f32[12,128,256]{2,1,0:T(8,128)S(1)}) custom-call(s32[72]{0:T(128)S(1)} %select_reduce_fusion.eff, bf16[128,1536]{1,0:T(8,128)(2,1)S(1)} %bitcast.14, bf16[128,256]{1,0:T(8,128)(2,1)S(1)} %bitcast.20, bf16[8,128,256]{2,1,0:T(8,128)(2,1)S(1)} %all-to-all-done.1.a, bf16[8,128,256]{2,1,0:T(8,128)(2,1)S(1)} %copy-done.1), custom_call_target="tpu_custom_call" | custom-call | flops 6000000000 | bytes 1024 | tf_op jit(solution)/shard_map/pallas_call | solution.py:129
  73.7 1.1 collective-permute-done.1.a
  74.8 2.5 %collective-permute-start.2 = (bf16[8,128,256]{2,1,0:T(8,128)(2,1)S(1)}, bf16[8,128,256]{2,1,0:T(8,128)(2,1)S(1)}, u32[]{:S(2)}, u32[]{:S(2)}) collective-permute-start(bf16[8,128,256]{2,1,0:T(8,128)(2,1)S(1)} %collective-permute-done.1.a), channel_id=1, source_target_pairs={{256,264},{264,256},{384,392},{392,384},{257,265},{265,257},{385,3... | collective-permute-start | bytes 1572872 | tf_op jit(solution)/shard_map/ppermute | solution.py:180
  77.3 0.0 collective-permute-done.5.b
  77.3 3.7 %shard_map.57 = (f32[12,128,128]{2,1,0:T(8,128)S(1)}, f32[12,128,256]{2,1,0:T(8,128)S(1)}) custom-call(s32[72]{0:T(128)S(1)} %select_reduce_fusion.eff, bf16[128,1536]{1,0:T(8,128)(2,1)S(1)} %bitcast.15, bf16[8,128,256]{2,1,0:T(8,128)(2,1)S(1)} %collective-permute-done.a, bf16[8,128,256]{2,1,0:T(8,128)(2,1)S(1)} %collective-permute-done.5.b, ...), custom_call_target="tpu_custom_call" | custom-call | flops 5000000000 | bytes 1024 | tf_op jit(solution)/shard_map/pallas_call | solution.py:141
  81.0 0.0 collective-permute-done.4.b
  81.0 5.0 %shard_map.58 = (f32[12,128,128]{2,1,0:T(8,128)S(1)}, f32[12,128,256]{2,1,0:T(8,128)S(1)}) custom-call(s32[72]{0:T(128)S(1)} %select_reduce_fusion.eff, bf16[128,1536]{1,0:T(8,128)(2,1)S(1)} %bitcast.16, bf16[8,128,256]{2,1,0:T(8,128)(2,1)S(1)} %collective-permute-done.3.a, bf16[8,128,256]{2,1,0:T(8,128)(2,1)} %collective-permute-done.4.b, ...), custom_call_target="tpu_custom_call" | custom-call | flops 5000000000 | bytes 1024 | tf_op jit(solution)/shard_map/pallas_call | solution.py:141
  86.0 0.0 collective-permute-done.2.b
  86.0 3.7 %shard_map.59 = bf16[128,1536]{1,0:T(8,128)(2,1)S(1)} custom-call(s32[72]{0:T(128)S(1)} %select_reduce_fusion.eff, bf16[128,1536]{1,0:T(8,128)(2,1)S(1)} %bitcast.17, bf16[8,128,256]{2,1,0:T(8,128)(2,1)S(1)} %collective-permute-done.1.a, bf16[8,128,256]{2,1,0:T(8,128)(2,1)S(1)} %collective-permute-done.2.b, f32[12,128,128]{2,1,0:T(8,128)S(1)} %get-tuple-element.21.m_in, ...), custom_call_target="tpu_custom_call" | custom-call | flops 4000000000 | bytes 1024 | tf_op jit(solution)/shard_map/pallas_call | solution.py:153
  89.8 21.5 %all_to_all.21 = bf16[8,16,1536]{2,1,0:T(8,128)(2,1)S(1)} all-to-all(bf16[8,16,1536]{2,1,0:T(8,128)(2,1)S(1)} %bitcast.18), channel_id=1, replica_groups=mesh['x'=4,'z'=8,'c'=2,'t'=8] {'t'}, dimensions={0} | all-to-all | bytes 786432 | tf_op jit(solution)/shard_map/all_to_all | solution.py:245
  111.3 0.8 copy.11
  (10 shorter events, 0.0 us)
Async XLA Ops:
  0.0 28.1 %copy-start.2 = (bf16[16,12288]{1,0:T(8,128)(2,1)S(1)}, bf16[16,12288]{1,0:T(8,128)(2,1)}, u32[]{:S(2)}) copy-start(bf16[16,12288]{1,0:T(8,128)(2,1)} %param.5) | copy-start | bytes 1179652
  0.0 28.9 %copy-start.4 = (s32[1,52]{1,0:T(1,128)S(1)}, s32[1,52]{1,0:T(1,128)}, u32[]{:S(2)}) copy-start(s32[1,52]{1,0:T(1,128)} %param.9) | copy-start | bytes 628
  0.0 29.0 %copy-start.3 = (s32[64]{0:T(128)S(1)}, s32[64]{0:T(128)}, u32[]{:S(2)}) copy-start(s32[64]{0:T(128)} %param.8) | copy-start | bytes 772
  17.8 26.4 %all-to-all-start.1 = ((bf16[8,128,256]{2,1,0:T(8,128)(2,1)}), bf16[8,128,256]{2,1,0:T(8,128)(2,1)S(1)}, u32[]{:S(2)}, u32[]{:S(2)}) async-start(bf16[8,128,256]{2,1,0:T(8,128)(2,1)} %broadcast_in_dim.50), calls=%async_computation.1 | async-start | bytes 1048576 | tf_op jit(solution)/shard_map/all_to_all | solution.py:226
  44.2 25.0 %all-to-all-start.2 = ((bf16[8,16,1536]{2,1,0:T(8,128)(2,1)}), bf16[8,16,1536]{2,1,0:T(8,128)(2,1)S(1)}, u32[]{:S(2)}, u32[]{:S(2)}) async-start(bf16[8,16,1536]{2,1,0:T(8,128)(2,1)} %bitcast.13), calls=%async_computation.2 | async-start | bytes 786432 | tf_op jit(solution)/shard_map/all_to_all | solution.py:231
  47.6 14.2 %collective-permute-start = (bf16[8,128,256]{2,1,0:T(8,128)(2,1)S(1)}, bf16[8,128,256]{2,1,0:T(8,128)(2,1)S(1)}, u32[]{:S(2)}, u32[]{:S(2)}) collective-permute-start(bf16[8,128,256]{2,1,0:T(8,128)(2,1)S(1)} %all-to-all-done.1.a), channel_id=1, source_target_pairs={{0,128},{8,392},{128,256},{136,8},{256,384},{1,129},{9,393},{129,2... | collective-permute-start | bytes 1572872 | tf_op jit(solution)/shard_map/ppermute | solution.py:175
  48.9 16.1 %collective-permute-start.3 = (bf16[8,128,256]{2,1,0:T(8,128)(2,1)S(1)}, bf16[8,128,256]{2,1,0:T(8,128)(2,1)S(1)}, u32[]{:S(2)}, u32[]{:S(2)}) collective-permute-start(bf16[8,128,256]{2,1,0:T(8,128)(2,1)S(1)} %all-to-all-done.1.a), channel_id=1, source_target_pairs={{0,384},{8,136},{136,264},{264,392},{1,385},{9,137},{137,265},{265... | collective-permute-start | bytes 1572872 | tf_op jit(solution)/shard_map/ppermute | solution.py:175
  50.2 18.1 %collective-permute-start.6 = (bf16[8,128,256]{2,1,0:T(8,128)(2,1)S(1)}, bf16[8,128,256]{2,1,0:T(8,128)(2,1)S(1)}, u32[]{:S(2)}, u32[]{:S(2)}) collective-permute-start(bf16[8,128,256]{2,1,0:T(8,128)(2,1)S(1)} %all-to-all-done.1.a), channel_id=1, source_target_pairs={{0,8},{8,0},{1,9},{9,1},{2,10},{10,2},{3,11},{11,3},{4,12},{12,4},... | collective-permute-start | bytes 1572872 | tf_op jit(solution)/shard_map/ppermute | solution.py:165
  61.8 15.5 %collective-permute-start.5 = (bf16[8,128,256]{2,1,0:T(8,128)(2,1)S(1)}, bf16[8,128,256]{2,1,0:T(8,128)(2,1)S(1)}, u32[]{:S(2)}, u32[]{:S(2)}) collective-permute-start(bf16[8,128,256]{2,1,0:T(8,128)(2,1)S(1)} %collective-permute-done.a), channel_id=1, source_target_pairs={{128,136},{136,128},{256,264},{264,256},{384,392},{392,384},{129,1... | collective-permute-start | bytes 1572872 | tf_op jit(solution)/shard_map/ppermute | solution.py:180
  63.7 11.1 %collective-permute-start.1 = (bf16[8,128,256]{2,1,0:T(8,128)(2,1)S(1)}, bf16[8,128,256]{2,1,0:T(8,128)(2,1)S(1)}, u32[]{:S(2)}, u32[]{:S(2)}) collective-permute-start(bf16[8,128,256]{2,1,0:T(8,128)(2,1)S(1)} %collective-permute-done.a), channel_id=1, source_target_pairs={{8,392},{128,256},{256,384},{392,264},{9,393},{129,257},{257,385},... | collective-permute-start | bytes 1572872 | tf_op jit(solution)/shard_map/ppermute | solution.py:175
  65.1 15.9 %collective-permute-start.4 = (bf16[8,128,256]{2,1,0:T(8,128)(2,1)S(1)}, bf16[8,128,256]{2,1,0:T(8,128)(2,1)}, u32[]{:S(2)}, u32[]{:S(2)}) collective-permute-start(bf16[8,128,256]{2,1,0:T(8,128)(2,1)S(1)} %collective-permute-done.3.a), channel_id=1, source_target_pairs={{128,136},{136,128},{256,264},{264,256},{384,392},{392,384},{129,1... | collective-permute-start | bytes 1572872 | tf_op jit(solution)/shard_map/ppermute | solution.py:180
  68.4 0.8 copy-start
  69.1 1.0 copy-start.1
  74.8 11.2 %collective-permute-start.2 = (bf16[8,128,256]{2,1,0:T(8,128)(2,1)S(1)}, bf16[8,128,256]{2,1,0:T(8,128)(2,1)S(1)}, u32[]{:S(2)}, u32[]{:S(2)}) collective-permute-start(bf16[8,128,256]{2,1,0:T(8,128)(2,1)S(1)} %collective-permute-done.1.a), channel_id=1, source_target_pairs={{256,264},{264,256},{384,392},{392,384},{257,265},{265,257},{385,3... | collective-permute-start | bytes 1572872 | tf_op jit(solution)/shard_map/ppermute | solution.py:180

commit v3 on v2

--- a/solution.py
+++ b/solution.py
@@ -15,8 +15,9 @@
 GROUP = HEADS // KV
 NX, NZ, NC, NT = 4, 8, 2, 8
 BIG = -1e30
+OWN = 64
 STEP = 16
-WIDE = 512
+WIDE = 1024
 LOG2E = 1.4426950408889634
 SCALE2 = LOG2E / math.sqrt(HD)
 F32 = jnp.float32
@@ -46,13 +47,14 @@
         m_ref[h] = top
 
 
-def far_tiles(eff_ref, base, q_ref, kv_refs, packed, bias, m_ref, acc_ref):
+def far_tiles(eff_ref, q_ref, copies, kv_refs, packed, bias, m_ref, acc_ref):
     row = lax.broadcasted_iota(jnp.int32, (TILE, HD), 0)
     lane = lax.broadcasted_iota(jnp.int32, (TILE, HD), 1)
     one = jnp.where(lane == 0, 1.0, 0.0).astype(BF16)
     count = jnp.int32(0)
-    slot = base
-    for kv_ref in kv_refs:
+    slot = 0
+    for copy, kv_ref in zip(copies, kv_refs):
+        copy.wait()
         for i in range(kv_ref.shape[0]):
             valid = eff_ref[slot]
             at = pl.ds(pl.multiple_of(count, STEP), TILE)
@@ -65,7 +67,7 @@
     bias[at, :] = jnp.full((WIDE, HD), BIG, BF16)
 
     def block(start, size):
-        at = pl.ds(pl.multiple_of(start, WIDE // 2), size)
+        at = pl.ds(pl.multiple_of(start, WIDE // 4), size)
         key_t = jnp.concatenate([packed[at, :HD].T, bias[at, :].T], axis=0)
         vext = jnp.concatenate([packed[at, HD:], jnp.ones((size, HD), BF16)], axis=1)
         for h in range(GROUP):
@@ -79,29 +81,29 @@
         block(k * WIDE, WIDE)
         return carry
 
-    wide = lax.div(count + (WIDE // 2 - 1), WIDE)
+    wide = lax.div(count + (WIDE // 4 - 1), WIDE)
     lax.fori_loop(0, wide, step, 0)
-
-    @pl.when(count > wide * WIDE)
+    done = wide * WIDE
+    rest = count - done
+    half = rest > WIDE // 4
+
+    @pl.when(half)
     def _():
-        block(wide * WIDE, WIDE // 2)
-
-
-def first_kernel(base, eff, q, own, a, b, m, acc, packed, bias):
-    own_tile(eff[64], q, own, m, acc)
-    far_tiles(eff, base, q, (a, b), packed, bias, m, acc)
-
-
-def middle_kernel(base, eff, q, a, b, m_in, acc_in, m, acc, packed, bias):
-    m[...] = m_in[...]
-    acc[...] = acc_in[...]
-    far_tiles(eff, base, q, (a, b), packed, bias, m, acc)
-
-
-def last_kernel(base, eff, q, a, b, m_in, acc_in, out, m, acc, packed, bias):
-    m[...] = m_in[...]
-    acc[...] = acc_in[...]
-    far_tiles(eff, base, q, (a, b), packed, bias, m, acc)
+        block(done, WIDE // 2)
+
+    @pl.when((rest > WIDE // 2) | ((rest > 0) & jnp.logical_not(half)))
+    def _():
+        block(done + jnp.where(half, WIDE // 2, 0), WIDE // 4)
+
+
+def attend_kernel(eff, q, own, *refs):
+    *kv, out, here, m, acc, packed, bias, sems = refs
+    here = [here.at[i] for i in range(len(kv))]
+    copies = [pltpu.make_async_copy(a, b, sems.at[i]) for i, (a, b) in enumerate(zip(kv, here))]
+    for copy in copies:
+        copy.start()
+    own_tile(eff[OWN], q, own, m, acc)
+    far_tiles(eff, q, copies, here, packed, bias, m, acc)
     for h in range(GROUP):
         val = acc[h]
         out[:, h * HD : (h + 1) * HD] = (val[:, :HD] / val[:, HD:]).astype(BF16)
@@ -109,13 +111,7 @@
 
 VM = pl.BlockSpec(memory_space=pltpu.VMEM)
 SM = pl.BlockSpec(memory_space=pltpu.SMEM)
-STATE = (
-    jax.ShapeDtypeStruct((GROUP, TILE, HD), F32),
-    jax.ShapeDtypeStruct((GROUP, TILE, 2 * HD), F32),
-)
-ROWS = 2 * NZ * TILE + WIDE
-WORK = [pltpu.VMEM((ROWS, 2 * HD), BF16), pltpu.VMEM((ROWS, HD), BF16)]
-PARAMS = pltpu.CompilerParams(vmem_limit_bytes=24 * 1024 * 1024)
+PARAMS = pltpu.CompilerParams(vmem_limit_bytes=22 * 1024 * 1024)
 
 
 def busy(us):
@@ -125,40 +121,24 @@
 LIGHT = pl.CostEstimate(flops=1, bytes_accessed=1, transcendentals=1)
 
 
-def first(base, eff, q, own, a, b):
+def attend(eff, q, own, *kv):
+    rows = len(kv) * NZ * TILE + WIDE
     return pl.pallas_call(
-        functools.partial(first_kernel, base),
-        out_shape=STATE,
-        in_specs=[SM, VM, VM, VM, VM],
-        out_specs=(VM, VM),
-        scratch_shapes=WORK,
+        attend_kernel,
+        out_shape=jax.ShapeDtypeStruct((TILE, GROUP * HD), BF16),
+        in_specs=[SM, VM, VM] + [pl.BlockSpec(memory_space=pl.ANY)] * len(kv),
+        out_specs=VM,
+        scratch_shapes=[
+            pltpu.VMEM((len(kv), NZ, TILE, 2 * HD), BF16),
+            pltpu.VMEM((GROUP, TILE, HD), F32),
+            pltpu.VMEM((GROUP, TILE, 2 * HD), F32),
+            pltpu.VMEM((rows, 2 * HD), BF16),
+            pltpu.VMEM((rows, HD), BF16),
+            pltpu.SemaphoreType.DMA((len(kv),)),
+        ],
         compiler_params=PARAMS,
-        cost_estimate=busy(6),
-    )(eff, q, own, a, b)
-
-
-def middle(base, eff, q, a, b, state):
-    return pl.pallas_call(
-        functools.partial(middle_kernel, base),
-        out_shape=STATE,
-        in_specs=[SM, VM, VM, VM, VM, VM],
-        out_specs=(VM, VM),
-        scratch_shapes=WORK,
-        compiler_params=PARAMS,
-        cost_estimate=busy(5),
-    )(eff, q, a, b, *state)
-
-
-def last(base, eff, q, a, b, state):
-    return pl.pallas_call(
-        functools.partial(last_kernel, base),
-        out_shape=jax.ShapeDtypeStruct((TILE, GROUP * HD), BF16),
-        in_specs=[SM, VM, VM, VM, VM, VM],
-        out_specs=VM,
-        scratch_shapes=[pltpu.VMEM(s.shape, s.dtype) for s in STATE] + WORK,
-        compiler_params=PARAMS,
-        cost_estimate=busy(4),
-    )(eff, q, a, b, *state)
+        cost_estimate=busy(10),
+    )(eff, q, own, *kv)
 
 
 def flip(a):
@@ -226,21 +206,18 @@
     line = lax.all_to_all(jnp.broadcast_to(own, (NZ, TILE, 2 * HD)), "z", 0, 0, tiled=True)
 
     eff = seen_lengths(tile_len, ancestors[0], x, z, c)
-    q = queries.reshape(rows, KV, GROUP * HD).transpose(1, 0, 2)
-    q, eff, line = barrier((q, eff, line))
-    q = lax.all_to_all(q, "t", 0, 0, tiled=True).reshape(TILE, GROUP * HD)
 
     p1 = along(line, 1, FIRST)
     p2 = along(line, -1, NEXT)
     c0 = flip(line)
-    state = first(0, eff, q, own, line, c0)
+    q = queries.reshape(rows, KV, GROUP * HD).transpose(1, 0, 2)
+    q, eff, c0 = barrier((q, eff, c0))
+    q = lax.all_to_all(q, "t", 0, 0, tiled=True).reshape(TILE, GROUP * HD)
     p3 = along(p1, 1, THIRD)
     c1 = flip_from(p1, 1)
-    state = middle(16, eff, q, p1, c1, state)
     c2 = flip_from(p2, 1)
     c3 = flip_from(p3, 2)
-    state = middle(32, eff, q, p2, c2, state)
-    out = last(48, eff, q, p3, c3, state)
+    out = attend(eff, q, own, line, c0, p1, c1, p2, c2, p3, c3)
 
     out = lax.all_to_all(out.reshape(NT, rows, GROUP * HD), "t", 0, 0, tiled=True)
     return out.transpose(1, 0, 2).reshape(rows, HEADS * HD)

time: 113 us -> 109 us (0.965)
  the two profiles are of different devices: /device:TPU:6 before, /device:TPU:5 now
where the time goes in v3:
time: 109 us; the launch traced here: 107 us
  blocking collectives  60.3 us (55%)
  starting transfers between devices  29.6 us (27%)
  Pallas kernels  10.7 us (10%)
  local copies, waits for them, and re-layouts  5.93 us (5%)
    all_to_all x1, blocking collectives, local(): lax.all_to_all(jnp.broadcast_to(own, (NZ, TILE, 2 * HD)), 'z', 0, 0, tile...  24.4 us
    all_to_all x1, blocking collectives, local(): lax.all_to_all(out.reshape(NT, rows, GROUP * HD), 't', 0, 0, tiled=True)  21.9 us
    all_to_all x1, blocking collectives, local(): lax.all_to_all(spread(keys, values), 't', 0, 0, tiled=True)  14.1 us
    ppermute x3, starting transfers between devices, flip_from(): return lax.ppermute(a, ('x', 'c'), pairs)  13.9 us
    pallas_call x1, Pallas kernels, attend(): pl.pallas_call(attend_kernel, out_shape=jax.ShapeDtypeStruct((TILE, GROUP...  9.33 us
    ppermute x1, starting transfers between devices, flip(): return lax.ppermute(a, 'c', [(0, 1), (1, 0)])  8.32 us
    unnamed x14, local copies, waits for them, and re-layouts  4.35 us
    ppermute x3, starting transfers between devices, along(): return lax.ppermute(a, ('x', 'c'), pairs)  3.9 us
  transfers between devices with their start and end apart: 8, of which 0 were waited for; matrix products, arithmetic and copies ran while one was open for 1% of the time, Pallas kernels for 0%

profile of v3, /device:TPU:5, one launch (start us, length us, event | category | flops | bytes accessed | tf_op | source)
XLA Modules:
  0.0 107.0 jit_solution(16975144522543030870)
XLA Ops:
  0.0 1.4 %shard_map.55 = bf16[8,16,256]{2,1,0:T(8,128)(2,1)} custom-call(bf16[16,1024]{1,0:T(8,128)(2,1)} %k.1, bf16[16,1024]{1,0:T(8,128)(2,1)} %v.1), custom_call_target="tpu_custom_call" | custom-call | flops 1 | bytes 1 | tf_op jit(solution)/shard_map/pallas_call | solution.py:192
  1.4 14.1 %all_to_all.20 = bf16[8,16,256]{2,1,0:T(8,128)(2,1)S(1)} all-to-all(bf16[8,16,256]{2,1,0:T(8,128)(2,1)} %shard_map.55), channel_id=1, replica_groups=mesh['x'=4,'z'=8,'c'=2,'t'=8] {'t'}, dimensions={0} | all-to-all | bytes 131072 | tf_op jit(solution)/shard_map/all_to_all | solution.py:205
  15.5 0.0 copy-start.4
  15.5 24.4 %all_to_all.21.refs_0_ = bf16[8,128,256]{2,1,0:T(8,128)(2,1)S(1)} all-to-all(bf16[8,128,256]{2,1,0:T(8,128)(2,1)S(1)} %broadcast_in_dim.50), channel_id=1, replica_groups=mesh['x'=4,'z'=8,'c'=2,'t'=8] {'z'}, dimensions={0} | all-to-all | bytes 1048576 | tf_op jit(solution)/shard_map/all_to_all | solution.py:206
  39.9 0.7 collective-permute-start.1
  40.6 8.3 %collective-permute-start = (bf16[8,128,256]{2,1,0:T(8,128)(2,1)S(1)}, bf16[8,128,256]{2,1,0:T(8,128)(2,1)S(1)}, u32[]{:S(2)}, u32[]{:S(2)}) collective-permute-start(bf16[8,128,256]{2,1,0:T(8,128)(2,1)S(1)} %all_to_all.21.refs_0_), channel_id=1, source_target_pairs={{0,8},{8,0},{1,9},{9,1},{2,10},{10,2},{3,11},{11,3},{4,12},{12,4},... | collective-permute-start | bytes 1572872 | tf_op jit(solution)/shard_map/ppermute | solution.py:145
  49.0 0.0 copy-start.6
  49.0 1.9 %collective-permute-start.3 = (bf16[8,128,256]{2,1,0:T(8,128)(2,1)S(1)}, bf16[8,128,256]{2,1,0:T(8,128)(2,1)S(1)}, u32[]{:S(2)}, u32[]{:S(2)}) collective-permute-start(bf16[8,128,256]{2,1,0:T(8,128)(2,1)S(1)} %all_to_all.21.refs_0_), channel_id=1, source_target_pairs={{0,384},{8,136},{136,264},{264,392},{1,385},{9,137},{137,265},{265... | collective-permute-start | bytes 1572872 | tf_op jit(solution)/shard_map/ppermute | solution.py:155
  50.9 0.0 collective-permute-done.1.refs_2_
  50.9 1.3 %collective-permute-start.5 = (bf16[8,128,256]{2,1,0:T(8,128)(2,1)S(1)}, bf16[8,128,256]{2,1,0:T(8,128)(2,1)S(1)}, u32[]{:S(2)}, u32[]{:S(2)}) collective-permute-start(bf16[8,128,256]{2,1,0:T(8,128)(2,1)S(1)} %collective-permute-done.1.refs_2_), channel_id=1, source_target_pairs={{8,392},{128,256},{256,384},{392,264},{9,393},{129,257},{257,385},... | collective-permute-start | bytes 1572872 | tf_op jit(solution)/shard_map/ppermute | solution.py:155
  52.3 0.1 compare_reduce_fusion
  52.4 0.8 copy.13
  53.1 0.6 copy-done.5
  53.8 0.1 select_reduce_fusion.eff
  53.9 0.0 collective-permute-done.refs_1_
  53.9 3.5 %all-to-all-start.2 = ((bf16[8,16,1536]{2,1,0:T(8,128)(2,1)}), bf16[8,16,1536]{2,1,0:T(8,128)(2,1)S(1)}, u32[]{:S(2)}, u32[]{:S(2)}) async-start(bf16[8,16,1536]{2,1,0:T(8,128)(2,1)} %bitcast.13), calls=%async_computation.2 | async-start | bytes 786432 | tf_op jit(solution)/shard_map/all_to_all | solution.py:215
  57.3 9.6 %collective-permute-start.2 = (bf16[8,128,256]{2,1,0:T(8,128)(2,1)S(1)}, bf16[8,128,256]{2,1,0:T(8,128)(2,1)S(1)}, u32[]{:S(2)}, u32[]{:S(2)}) collective-permute-start(bf16[8,128,256]{2,1,0:T(8,128)(2,1)S(1)} %collective-permute-done.1.refs_2_), channel_id=1, source_target_pairs={{128,136},{136,128},{256,264},{264,256},{384,392},{392,384},{129,1... | collective-permute-start | bytes 1572872 | tf_op jit(solution)/shard_map/ppermute | solution.py:160
  67.0 0.0 collective-permute-done.3.refs_4_
  67.0 1.9 %collective-permute-start.4 = (bf16[8,128,256]{2,1,0:T(8,128)(2,1)S(1)}, bf16[8,128,256]{2,1,0:T(8,128)(2,1)S(1)}, u32[]{:S(2)}, u32[]{:S(2)}) collective-permute-start(bf16[8,128,256]{2,1,0:T(8,128)(2,1)S(1)} %collective-permute-done.3.refs_4_), channel_id=1, source_target_pairs={{128,136},{136,128},{256,264},{264,256},{384,392},{392,384},{129,1... | collective-permute-start | bytes 1572872 | tf_op jit(solution)/shard_map/ppermute | solution.py:160
  68.9 0.0 collective-permute-done.5.refs_6_
  68.9 2.4 %collective-permute-start.6 = (bf16[8,128,256]{2,1,0:T(8,128)(2,1)S(1)}, bf16[8,128,256]{2,1,0:T(8,128)(2,1)}, u32[]{:S(2)}, u32[]{:S(2)}) collective-permute-start(bf16[8,128,256]{2,1,0:T(8,128)(2,1)S(1)} %collective-permute-done.5.refs_6_), channel_id=1, source_target_pairs={{256,264},{264,256},{384,392},{392,384},{257,265},{265,257},{385,3... | collective-permute-start | bytes 1572872 | tf_op jit(solution)/shard_map/ppermute | solution.py:160
  71.3 0.0 collective-permute-done.2.refs_3_
  71.4 0.8 copy-done
  72.1 0.0 collective-permute-done.4.refs_5_
  72.1 0.8 copy-done.2
  73.0 0.0 all-to-all-done.2
  73.0 0.0 collective-permute-done.6.refs_7_
  73.0 1.0 copy-done.1
  74.0 1.0 copy-done.3
  75.1 9.3 %shard_map.56 = bf16[128,1536]{1,0:T(8,128)(2,1)S(1)} custom-call(s32[72]{0:T(128)S(1)} %select_reduce_fusion.eff, bf16[128,1536]{1,0:T(8,128)(2,1)S(1)} %bitcast.14, bf16[128,256]{1,0:T(8,128)(2,1)S(1)} %bitcast.17, bf16[8,128,256]{2,1,0:T(8,128)(2,1)S(1)} %all_to_all.21.refs_0_, bf16[8,128,256]{2,1,0:T(8,128)(2,1)S(1)} %collective-permute-done.refs_1_, ...), custom_call_target="tpu_custom_call" | custom-call | flops 10000000000 | bytes 1024 | tf_op jit(solution)/shard_map/pallas_call | solution.py:126
  84.4 21.9 %all_to_all.22 = bf16[8,16,1536]{2,1,0:T(8,128)(2,1)S(1)} all-to-all(bf16[8,16,1536]{2,1,0:T(8,128)(2,1)S(1)} %bitcast.15), channel_id=1, replica_groups=mesh['x'=4,'z'=8,'c'=2,'t'=8] {'t'}, dimensions={0} | all-to-all | bytes 786432 | tf_op jit(solution)/shard_map/all_to_all | solution.py:222
  106.3 0.8 copy.11
  (10 shorter events, 0.1 us)
Async XLA Ops:
  15.5 36.8 %copy-start.4 = (bf16[16,12288]{1,0:T(8,128)(2,1)S(1)}, bf16[16,12288]{1,0:T(8,128)(2,1)}, u32[]{:S(2)}) copy-start(bf16[16,12288]{1,0:T(8,128)(2,1)} %param.5) | copy-start | bytes 1179652
  39.9 11.0 %collective-permute-start.1 = (bf16[8,128,256]{2,1,0:T(8,128)(2,1)S(1)}, bf16[8,128,256]{2,1,0:T(8,128)(2,1)S(1)}, u32[]{:S(2)}, u32[]{:S(2)}) collective-permute-start(bf16[8,128,256]{2,1,0:T(8,128)(2,1)S(1)} %all_to_all.21.refs_0_), channel_id=1, source_target_pairs={{0,128},{8,392},{128,256},{136,8},{256,384},{1,129},{9,393},{129,2... | collective-permute-start | bytes 1572872 | tf_op jit(solution)/shard_map/ppermute | solution.py:155
  40.6 13.2 %collective-permute-start = (bf16[8,128,256]{2,1,0:T(8,128)(2,1)S(1)}, bf16[8,128,256]{2,1,0:T(8,128)(2,1)S(1)}, u32[]{:S(2)}, u32[]{:S(2)}) collective-permute-start(bf16[8,128,256]{2,1,0:T(8,128)(2,1)S(1)} %all_to_all.21.refs_0_), channel_id=1, source_target_pairs={{0,8},{8,0},{1,9},{9,1},{2,10},{10,2},{3,11},{11,3},{4,12},{12,4},... | collective-permute-start | bytes 1572872 | tf_op jit(solution)/shard_map/ppermute | solution.py:145
  49.0 3.3 %copy-start.6 = (s32[1,52]{1,0:T(1,128)S(1)}, s32[1,52]{1,0:T(1,128)}, u32[]{:S(2)}) copy-start(s32[1,52]{1,0:T(1,128)} %param.9) | copy-start | bytes 628
  49.0 18.0 %collective-permute-start.3 = (bf16[8,128,256]{2,1,0:T(8,128)(2,1)S(1)}, bf16[8,128,256]{2,1,0:T(8,128)(2,1)S(1)}, u32[]{:S(2)}, u32[]{:S(2)}) collective-permute-start(bf16[8,128,256]{2,1,0:T(8,128)(2,1)S(1)} %all_to_all.21.refs_0_), channel_id=1, source_target_pairs={{0,384},{8,136},{136,264},{264,392},{1,385},{9,137},{137,265},{265... | collective-permute-start | bytes 1572872 | tf_op jit(solution)/shard_map/ppermute | solution.py:155
  50.9 18.0 %collective-permute-start.5 = (bf16[8,128,256]{2,1,0:T(8,128)(2,1)S(1)}, bf16[8,128,256]{2,1,0:T(8,128)(2,1)S(1)}, u32[]{:S(2)}, u32[]{:S(2)}) collective-permute-start(bf16[8,128,256]{2,1,0:T(8,128)(2,1)S(1)} %collective-permute-done.1.refs_2_), channel_id=1, source_target_pairs={{8,392},{128,256},{256,384},{392,264},{9,393},{129,257},{257,385},... | collective-permute-start | bytes 1572872 | tf_op jit(solution)/shard_map/ppermute | solution.py:155
  53.1 0.7 copy-start.5
  53.9 19.1 %all-to-all-start.2 = ((bf16[8,16,1536]{2,1,0:T(8,128)(2,1)}), bf16[8,16,1536]{2,1,0:T(8,128)(2,1)S(1)}, u32[]{:S(2)}, u32[]{:S(2)}) async-start(bf16[8,16,1536]{2,1,0:T(8,128)(2,1)} %bitcast.13), calls=%async_computation.2 | async-start | bytes 786432 | tf_op jit(solution)/shard_map/all_to_all | solution.py:215
  57.3 14.0 %collective-permute-start.2 = (bf16[8,128,256]{2,1,0:T(8,128)(2,1)S(1)}, bf16[8,128,256]{2,1,0:T(8,128)(2,1)S(1)}, u32[]{:S(2)}, u32[]{:S(2)}) collective-permute-start(bf16[8,128,256]{2,1,0:T(8,128)(2,1)S(1)} %collective-permute-done.1.refs_2_), channel_id=1, source_target_pairs={{128,136},{136,128},{256,264},{264,256},{384,392},{392,384},{129,1... | collective-permute-start | bytes 1572872 | tf_op jit(solution)/shard_map/ppermute | solution.py:160
  67.0 5.1 %collective-permute-start.4 = (bf16[8,128,256]{2,1,0:T(8,128)(2,1)S(1)}, bf16[8,128,256]{2,1,0:T(8,128)(2,1)S(1)}, u32[]{:S(2)}, u32[]{:S(2)}) collective-permute-start(bf16[8,128,256]{2,1,0:T(8,128)(2,1)S(1)} %collective-permute-done.3.refs_4_), channel_id=1, source_target_pairs={{128,136},{136,128},{256,264},{264,256},{384,392},{392,384},{129,1... | collective-permute-start | bytes 1572872 | tf_op jit(solution)/shard_map/ppermute | solution.py:160
  68.9 4.1 %collective-permute-start.6 = (bf16[8,128,256]{2,1,0:T(8,128)(2,1)S(1)}, bf16[8,128,256]{2,1,0:T(8,128)(2,1)}, u32[]{:S(2)}, u32[]{:S(2)}) collective-permute-start(bf16[8,128,256]{2,1,0:T(8,128)(2,1)S(1)} %collective-permute-done.5.refs_6_), channel_id=1, source_target_pairs={{256,264},{264,256},{384,392},{392,384},{257,265},{265,257},{385,3... | collective-permute-start | bytes 1572872 | tf_op jit(solution)/shard_map/ppermute | solution.py:160
  71.3 0.8 copy-start
  72.1 0.8 copy-start.2
  73.0 1.0 copy-start.1
  74.0 1.0 copy-start.3

commit v4 on v3

--- a/solution.py
+++ b/solution.py
@@ -111,7 +111,7 @@
 
 VM = pl.BlockSpec(memory_space=pltpu.VMEM)
 SM = pl.BlockSpec(memory_space=pltpu.SMEM)
-PARAMS = pltpu.CompilerParams(vmem_limit_bytes=22 * 1024 * 1024)
+PARAMS = pltpu.CompilerParams(vmem_limit_bytes=50 * 1024 * 1024)
 
 
 def busy(us):

time: 109 us -> 108 us (level)
  the two profiles are of different devices: /device:TPU:5 before, /device:TPU:6 now
where the time goes in v4:
time: 108 us; the launch traced here: 107 us
  blocking collectives  60.4 us (56%)
  starting transfers between devices  15.5 us (14%)
  Pallas kernels  14 us (13%)
  waiting for transfers between devices  13 us (12%)
  local copies, waits for them, and re-layouts  4.08 us (4%)
    all_to_all x1, blocking collectives, local(): lax.all_to_all(jnp.broadcast_to(own, (NZ, TILE, 2 * HD)), 'z', 0, 0, tile...  26.3 us
    all_to_all x1, blocking collectives, local(): lax.all_to_all(out.reshape(NT, rows, GROUP * HD), 't', 0, 0, tiled=True)  18.6 us
    all_to_all x1, blocking collectives, local(): lax.all_to_all(spread(keys, values), 't', 0, 0, tiled=True)  15.5 us
    pallas_call x1, Pallas kernels, attend(): pl.pallas_call(attend_kernel, out_shape=jax.ShapeDtypeStruct((TILE, GROUP...  12.6 us
    ppermute x3, waiting for transfers between devices, along(): return lax.ppermute(a, ('x', 'c'), pairs)  8.76 us
    ppermute x3, starting transfers between devices, flip_from(): return lax.ppermute(a, ('x', 'c'), pairs)  6.24 us
    all_to_all x1, waiting for transfers between devices, local(): q = lax.all_to_all(q, 't', 0, 0, tiled=True).reshape(TILE, GROUP * HD)  4.28 us
    ppermute x3, starting transfers between devices, along(): return lax.ppermute(a, ('x', 'c'), pairs)  3.85 us
  transfers between devices with their start and end apart: 8, of which 3 were waited for; matrix products, arithmetic and copies ran while one was open for 1% of the time, Pallas kernels for 0%

profile of v4, /device:TPU:6, one launch (start us, length us, event | category | flops | bytes accessed | tf_op | source)
XLA Modules:
  0.0 107.4 jit_solution(2385193165263013396)
XLA Ops:
  0.0 1.4 %shard_map.55 = bf16[8,16,256]{2,1,0:T(8,128)(2,1)} custom-call(bf16[16,1024]{1,0:T(8,128)(2,1)} %k.1, bf16[16,1024]{1,0:T(8,128)(2,1)} %v.1), custom_call_target="tpu_custom_call" | custom-call | flops 1 | bytes 1 | tf_op jit(solution)/shard_map/pallas_call | solution.py:192
  1.4 15.5 %all_to_all.20 = bf16[8,16,256]{2,1,0:T(8,128)(2,1)S(1)} all-to-all(bf16[8,16,256]{2,1,0:T(8,128)(2,1)} %shard_map.55), channel_id=1, replica_groups=mesh['x'=4,'z'=8,'c'=2,'t'=8] {'t'}, dimensions={0} | all-to-all | bytes 131072 | tf_op jit(solution)/shard_map/all_to_all | solution.py:205
  16.9 0.0 copy-start.2
  16.9 26.3 %all_to_all.21.refs_0_ = bf16[8,128,256]{2,1,0:T(8,128)(2,1)S(1)} all-to-all(bf16[8,128,256]{2,1,0:T(8,128)(2,1)S(1)} %broadcast_in_dim.50), channel_id=1, replica_groups=mesh['x'=4,'z'=8,'c'=2,'t'=8] {'z'}, dimensions={0} | all-to-all | bytes 1048576 | tf_op jit(solution)/shard_map/all_to_all | solution.py:206
  43.3 1.3 %collective-permute-start.1 = (bf16[8,128,256]{2,1,0:T(8,128)(2,1)S(1)}, bf16[8,128,256]{2,1,0:T(8,128)(2,1)S(1)}, u32[]{:S(2)}, u32[]{:S(2)}) collective-permute-start(bf16[8,128,256]{2,1,0:T(8,128)(2,1)S(1)} %all_to_all.21.refs_0_), channel_id=1, source_target_pairs={{0,128},{8,392},{128,256},{136,8},{256,384},{1,129},{9,393},{129,2... | collective-permute-start | bytes 1572872 | tf_op jit(solution)/shard_map/ppermute | solution.py:155
  44.6 1.9 %collective-permute-start = (bf16[8,128,256]{2,1,0:T(8,128)(2,1)S(1)}, bf16[8,128,256]{2,1,0:T(8,128)(2,1)S(1)}, u32[]{:S(2)}, u32[]{:S(2)}) collective-permute-start(bf16[8,128,256]{2,1,0:T(8,128)(2,1)S(1)} %all_to_all.21.refs_0_), channel_id=1, source_target_pairs={{0,8},{8,0},{1,9},{9,1},{2,10},{10,2},{3,11},{11,3},{4,12},{12,4},... | collective-permute-start | bytes 1572872 | tf_op jit(solution)/shard_map/ppermute | solution.py:145
  46.5 0.0 copy-start.4
  46.5 1.3 %collective-permute-start.3 = (bf16[8,128,256]{2,1,0:T(8,128)(2,1)S(1)}, bf16[8,128,256]{2,1,0:T(8,128)(2,1)S(1)}, u32[]{:S(2)}, u32[]{:S(2)}) collective-permute-start(bf16[8,128,256]{2,1,0:T(8,128)(2,1)S(1)} %all_to_all.21.refs_0_), channel_id=1, source_target_pairs={{0,384},{8,136},{136,264},{264,392},{1,385},{9,137},{137,265},{265... | collective-permute-start | bytes 1572872 | tf_op jit(solution)/shard_map/ppermute | solution.py:155
  47.8 8.3 %collective-permute-done.1.refs_2_ = bf16[8,128,256]{2,1,0:T(8,128)(2,1)S(1)} collective-permute-done((bf16[8,128,256]{2,1,0:T(8,128)(2,1)S(1)}, bf16[8,128,256]{2,1,0:T(8,128)(2,1)S(1)}, u32[]{:S(2)}, u32[]{:S(2)}) %collective-permute-start.1) | collective-permute-done | bytes 524320 | tf_op jit(solution)/shard_map/ppermute | solution.py:155
  56.2 1.3 %collective-permute-start.5 = (bf16[8,128,256]{2,1,0:T(8,128)(2,1)S(1)}, bf16[8,128,256]{2,1,0:T(8,128)(2,1)}, u32[]{:S(2)}, u32[]{:S(2)}) collective-permute-start(bf16[8,128,256]{2,1,0:T(8,128)(2,1)S(1)} %collective-permute-done.1.refs_2_), channel_id=1, source_target_pairs={{8,392},{128,256},{256,384},{392,264},{9,393},{129,257},{257,385},... | collective-permute-start | bytes 1572872 | tf_op jit(solution)/shard_map/ppermute | solution.py:155
  57.5 0.0 copy-done.4
  57.5 0.1 compare_reduce_fusion
  57.6 0.8 copy.13
  58.3 0.6 copy-done.3
  59.0 0.1 select_reduce_fusion.eff
  59.1 0.0 collective-permute-done.refs_1_
  59.1 3.5 %all-to-all-start.2 = ((bf16[8,16,1536]{2,1,0:T(8,128)(2,1)}), bf16[8,16,1536]{2,1,0:T(8,128)(2,1)S(1)}, u32[]{:S(2)}, u32[]{:S(2)}) async-start(bf16[8,16,1536]{2,1,0:T(8,128)(2,1)} %bitcast.13), calls=%async_computation.2 | async-start | bytes 786432 | tf_op jit(solution)/shard_map/all_to_all | solution.py:215
  62.6 1.9 %collective-permute-start.2 = (bf16[8,128,256]{2,1,0:T(8,128)(2,1)S(1)}, bf16[8,128,256]{2,1,0:T(8,128)(2,1)S(1)}, u32[]{:S(2)}, u32[]{:S(2)}) collective-permute-start(bf16[8,128,256]{2,1,0:T(8,128)(2,1)S(1)} %collective-permute-done.1.refs_2_), channel_id=1, source_target_pairs={{128,136},{136,128},{256,264},{264,256},{384,392},{392,384},{129,1... | collective-permute-start | bytes 1572872 | tf_op jit(solution)/shard_map/ppermute | solution.py:160
  64.5 0.0 collective-permute-done.3.refs_4_
  64.5 2.4 %collective-permute-start.4 = (bf16[8,128,256]{2,1,0:T(8,128)(2,1)S(1)}, bf16[8,128,256]{2,1,0:T(8,128)(2,1)S(1)}, u32[]{:S(2)}, u32[]{:S(2)}) collective-permute-start(bf16[8,128,256]{2,1,0:T(8,128)(2,1)S(1)} %collective-permute-done.3.refs_4_), channel_id=1, source_target_pairs={{128,136},{136,128},{256,264},{264,256},{384,392},{392,384},{129,1... | collective-permute-start | bytes 1572872 | tf_op jit(solution)/shard_map/ppermute | solution.py:160
  66.9 0.4 collective-permute-done.5.refs_6_
  67.3 1.9 %collective-permute-start.6 = (bf16[8,128,256]{2,1,0:T(8,128)(2,1)}, bf16[8,128,256]{2,1,0:T(8,128)(2,1)}, u32[]{:S(2)}, u32[]{:S(2)}) collective-permute-start(bf16[8,128,256]{2,1,0:T(8,128)(2,1)} %collective-permute-done.5.refs_6_), channel_id=1, source_target_pairs={{256,264},{264,256},{384,392},{392,384},{257,265},{265,257},{385,3... | collective-permute-start | bytes 1572872 | tf_op jit(solution)/shard_map/ppermute | solution.py:160
  69.3 0.0 collective-permute-done.2.refs_3_
  69.3 0.0 collective-permute-done.4.refs_5_
  69.3 0.0 copy-start
  69.3 0.8 copy-done
  70.1 4.3 %all-to-all-done.2 = bf16[8,16,1536]{2,1,0:T(8,128)(2,1)S(1)} async-done(((bf16[8,16,1536]{2,1,0:T(8,128)(2,1)}), bf16[8,16,1536]{2,1,0:T(8,128)(2,1)S(1)}, u32[]{:S(2)}, u32[]{:S(2)}) %all-to-all-start.2) | async-done | bytes 393248 | tf_op jit(solution)/shard_map/all_to_all | solution.py:215
  74.4 0.0 collective-permute-done.6.refs_7_
  74.4 1.0 copy-done.1
  75.4 12.6 %shard_map.56 = bf16[128,1536]{1,0:T(8,128)(2,1)S(1)} custom-call(s32[72]{0:T(128)S(1)} %select_reduce_fusion.eff, bf16[128,1536]{1,0:T(8,128)(2,1)S(1)} %bitcast.14, bf16[128,256]{1,0:T(8,128)(2,1)S(1)} %bitcast.17, bf16[8,128,256]{2,1,0:T(8,128)(2,1)S(1)} %all_to_all.21.refs_0_, bf16[8,128,256]{2,1,0:T(8,128)(2,1)S(1)} %collective-permute-done.refs_1_, ...), custom_call_target="tpu_custom_call" | custom-call | flops 10000000000 | bytes 1024 | tf_op jit(solution)/shard_map/pallas_call | solution.py:126
  88.0 18.6 %all_to_all.22 = bf16[8,16,1536]{2,1,0:T(8,128)(2,1)S(1)} all-to-all(bf16[8,16,1536]{2,1,0:T(8,128)(2,1)S(1)} %bitcast.15), channel_id=1, replica_groups=mesh['x'=4,'z'=8,'c'=2,'t'=8] {'t'}, dimensions={0} | all-to-all | bytes 786432 | tf_op jit(solution)/shard_map/all_to_all | solution.py:222
  106.6 0.8 copy.11
  (6 shorter events, 0.1 us)
Async XLA Ops:
  16.9 40.6 %copy-start.2 = (bf16[16,12288]{1,0:T(8,128)(2,1)S(1)}, bf16[16,12288]{1,0:T(8,128)(2,1)}, u32[]{:S(2)}) copy-start(bf16[16,12288]{1,0:T(8,128)(2,1)} %param.5) | copy-start | bytes 1179652
  43.3 12.9 %collective-permute-start.1 = (bf16[8,128,256]{2,1,0:T(8,128)(2,1)S(1)}, bf16[8,128,256]{2,1,0:T(8,128)(2,1)S(1)}, u32[]{:S(2)}, u32[]{:S(2)}) collective-permute-start(bf16[8,128,256]{2,1,0:T(8,128)(2,1)S(1)} %all_to_all.21.refs_0_), channel_id=1, source_target_pairs={{0,128},{8,392},{128,256},{136,8},{256,384},{1,129},{9,393},{129,2... | collective-permute-start | bytes 1572872 | tf_op jit(solution)/shard_map/ppermute | solution.py:155
  44.6 14.5 %collective-permute-start = (bf16[8,128,256]{2,1,0:T(8,128)(2,1)S(1)}, bf16[8,128,256]{2,1,0:T(8,128)(2,1)S(1)}, u32[]{:S(2)}, u32[]{:S(2)}) collective-permute-start(bf16[8,128,256]{2,1,0:T(8,128)(2,1)S(1)} %all_to_all.21.refs_0_), channel_id=1, source_target_pairs={{0,8},{8,0},{1,9},{9,1},{2,10},{10,2},{3,11},{11,3},{4,12},{12,4},... | collective-permute-start | bytes 1572872 | tf_op jit(solution)/shard_map/ppermute | solution.py:145
  46.5 10.9 %copy-start.4 = (s32[1,52]{1,0:T(1,128)S(1)}, s32[1,52]{1,0:T(1,128)}, u32[]{:S(2)}) copy-start(s32[1,52]{1,0:T(1,128)} %param.9) | copy-start | bytes 628
  46.5 18.0 %collective-permute-start.3 = (bf16[8,128,256]{2,1,0:T(8,128)(2,1)S(1)}, bf16[8,128,256]{2,1,0:T(8,128)(2,1)S(1)}, u32[]{:S(2)}, u32[]{:S(2)}) collective-permute-start(bf16[8,128,256]{2,1,0:T(8,128)(2,1)S(1)} %all_to_all.21.refs_0_), channel_id=1, source_target_pairs={{0,384},{8,136},{136,264},{264,392},{1,385},{9,137},{137,265},{265... | collective-permute-start | bytes 1572872 | tf_op jit(solution)/shard_map/ppermute | solution.py:155
  56.2 11.2 %collective-permute-start.5 = (bf16[8,128,256]{2,1,0:T(8,128)(2,1)S(1)}, bf16[8,128,256]{2,1,0:T(8,128)(2,1)}, u32[]{:S(2)}, u32[]{:S(2)}) collective-permute-start(bf16[8,128,256]{2,1,0:T(8,128)(2,1)S(1)} %collective-permute-done.1.refs_2_), channel_id=1, source_target_pairs={{8,392},{128,256},{256,384},{392,264},{9,393},{129,257},{257,385},... | collective-permute-start | bytes 1572872 | tf_op jit(solution)/shard_map/ppermute | solution.py:155
  58.3 0.7 copy-start.3
  59.1 15.3 %all-to-all-start.2 = ((bf16[8,16,1536]{2,1,0:T(8,128)(2,1)}), bf16[8,16,1536]{2,1,0:T(8,128)(2,1)S(1)}, u32[]{:S(2)}, u32[]{:S(2)}) async-start(bf16[8,16,1536]{2,1,0:T(8,128)(2,1)} %bitcast.13), calls=%async_computation.2 | async-start | bytes 786432 | tf_op jit(solution)/shard_map/all_to_all | solution.py:215
  62.6 6.7 %collective-permute-start.2 = (bf16[8,128,256]{2,1,0:T(8,128)(2,1)S(1)}, bf16[8,128,256]{2,1,0:T(8,128)(2,1)S(1)}, u32[]{:S(2)}, u32[]{:S(2)}) collective-permute-start(bf16[8,128,256]{2,1,0:T(8,128)(2,1)S(1)} %collective-permute-done.1.refs_2_), channel_id=1, source_target_pairs={{128,136},{136,128},{256,264},{264,256},{384,392},{392,384},{129,1... | collective-permute-start | bytes 1572872 | tf_op jit(solution)/shard_map/ppermute | solution.py:160
  64.5 4.8 %collective-permute-start.4 = (bf16[8,128,256]{2,1,0:T(8,128)(2,1)S(1)}, bf16[8,128,256]{2,1,0:T(8,128)(2,1)S(1)}, u32[]{:S(2)}, u32[]{:S(2)}) collective-permute-start(bf16[8,128,256]{2,1,0:T(8,128)(2,1)S(1)} %collective-permute-done.3.refs_4_), channel_id=1, source_target_pairs={{128,136},{136,128},{256,264},{264,256},{384,392},{392,384},{129,1... | collective-permute-start | bytes 1572872 | tf_op jit(solution)/shard_map/ppermute | solution.py:160
  67.3 7.0 %collective-permute-start.6 = (bf16[8,128,256]{2,1,0:T(8,128)(2,1)}, bf16[8,128,256]{2,1,0:T(8,128)(2,1)}, u32[]{:S(2)}, u32[]{:S(2)}) collective-permute-start(bf16[8,128,256]{2,1,0:T(8,128)(2,1)} %collective-permute-done.5.refs_6_), channel_id=1, source_target_pairs={{256,264},{264,256},{384,392},{392,384},{257,265},{265,257},{385,3... | collective-permute-start | bytes 1572872 | tf_op jit(solution)/shard_map/ppermute | solution.py:160
  69.3 0.8 copy-start
  74.4 1.0 copy-start.1

commit v5 on v4

--- a/solution.py
+++ b/solution.py
@@ -47,14 +47,13 @@
         m_ref[h] = top
 
 
-def far_tiles(eff_ref, q_ref, copies, kv_refs, packed, bias, m_ref, acc_ref):
+def far_tiles(eff_ref, base, q_ref, kv_refs, packed, bias, m_ref, acc_ref):
     row = lax.broadcasted_iota(jnp.int32, (TILE, HD), 0)
     lane = lax.broadcasted_iota(jnp.int32, (TILE, HD), 1)
     one = jnp.where(lane == 0, 1.0, 0.0).astype(BF16)
     count = jnp.int32(0)
-    slot = 0
-    for copy, kv_ref in zip(copies, kv_refs):
-        copy.wait()
+    slot = base
+    for kv_ref in kv_refs:
         for i in range(kv_ref.shape[0]):
             valid = eff_ref[slot]
             at = pl.ds(pl.multiple_of(count, STEP), TILE)
@@ -96,14 +95,17 @@
         block(done + jnp.where(half, WIDE // 2, 0), WIDE // 4)
 
 
-def attend_kernel(eff, q, own, *refs):
-    *kv, out, here, m, acc, packed, bias, sems = refs
-    here = [here.at[i] for i in range(len(kv))]
-    copies = [pltpu.make_async_copy(a, b, sems.at[i]) for i, (a, b) in enumerate(zip(kv, here))]
-    for copy in copies:
-        copy.start()
+def first_kernel(base, eff, q, own, *refs):
+    *kv, m, acc, packed, bias = refs
     own_tile(eff[OWN], q, own, m, acc)
-    far_tiles(eff, q, copies, here, packed, bias, m, acc)
+    far_tiles(eff, base, q, kv, packed, bias, m, acc)
+
+
+def last_kernel(base, eff, q, m_in, acc_in, *refs):
+    *kv, out, m, acc, packed, bias = refs
+    m[...] = m_in[...]
+    acc[...] = acc_in[...]
+    far_tiles(eff, base, q, kv, packed, bias, m, acc)
     for h in range(GROUP):
         val = acc[h]
         out[:, h * HD : (h + 1) * HD] = (val[:, :HD] / val[:, HD:]).astype(BF16)
@@ -111,7 +113,18 @@
 
 VM = pl.BlockSpec(memory_space=pltpu.VMEM)
 SM = pl.BlockSpec(memory_space=pltpu.SMEM)
-PARAMS = pltpu.CompilerParams(vmem_limit_bytes=50 * 1024 * 1024)
+STATE = (
+    jax.ShapeDtypeStruct((GROUP, TILE, HD), F32),
+    jax.ShapeDtypeStruct((GROUP, TILE, 2 * HD), F32),
+)
+
+
+def work(kv):
+    rows = sum(a.shape[0] for a in kv) * TILE + WIDE
+    return [pltpu.VMEM((rows, 2 * HD), BF16), pltpu.VMEM((rows, HD), BF16)]
+
+
+PARAMS = pltpu.CompilerParams(vmem_limit_bytes=24 * 1024 * 1024)
 
 
 def busy(us):
@@ -121,24 +134,28 @@
 LIGHT = pl.CostEstimate(flops=1, bytes_accessed=1, transcendentals=1)
 
 
-def attend(eff, q, own, *kv):
-    rows = len(kv) * NZ * TILE + WIDE
+def first(base, eff, q, own, *kv):
     return pl.pallas_call(
-        attend_kernel,
+        functools.partial(first_kernel, base),
+        out_shape=STATE,
+        in_specs=[SM, VM, VM] + [VM] * len(kv),
+        out_specs=(VM, VM),
+        scratch_shapes=work(kv),
+        compiler_params=PARAMS,
+        cost_estimate=busy(6),
+    )(eff, q, own, *kv)
+
+
+def last(base, eff, q, state, *kv):
+    return pl.pallas_call(
+        functools.partial(last_kernel, base),
         out_shape=jax.ShapeDtypeStruct((TILE, GROUP * HD), BF16),
-        in_specs=[SM, VM, VM] + [pl.BlockSpec(memory_space=pl.ANY)] * len(kv),
+        in_specs=[SM, VM, VM, VM] + [VM] * len(kv),
         out_specs=VM,
-        scratch_shapes=[
-            pltpu.VMEM((len(kv), NZ, TILE, 2 * HD), BF16),
-            pltpu.VMEM((GROUP, TILE, HD), F32),
-            pltpu.VMEM((GROUP, TILE, 2 * HD), F32),
-            pltpu.VMEM((rows, 2 * HD), BF16),
-            pltpu.VMEM((rows, HD), BF16),
-            pltpu.SemaphoreType.DMA((len(kv),)),
-        ],
+        scratch_shapes=[pltpu.VMEM(s.shape, s.dtype) for s in STATE] + work(kv),
         compiler_params=PARAMS,
-        cost_estimate=busy(10),
-    )(eff, q, own, *kv)
+        cost_estimate=busy(4),
+    )(eff, q, *state, *kv)
 
 
 def flip(a):
@@ -217,7 +234,8 @@
     c1 = flip_from(p1, 1)
     c2 = flip_from(p2, 1)
     c3 = flip_from(p3, 2)
-    out = attend(eff, q, own, line, c0, p1, c1, p2, c2, p3, c3)
+    state = first(0, eff, q, own, line, c0, p1, c1, p2, c2)
+    out = last(48, eff, q, state, p3, c3)
 
     out = lax.all_to_all(out.reshape(NT, rows, GROUP * HD), "t", 0, 0, tiled=True)
     return out.transpose(1, 0, 2).reshape(rows, HEADS * HD)

time: 108 us -> 112 us (1.037)
  blocking collectives: 60.4 us -> 33.9 us
  waiting for transfers between devices: 13 us -> 30.3 us
  starting transfers between devices: 15.5 us -> 25.8 us
  local copies, waits for them, and re-layouts: 4.08 us -> 6.08 us
    all_to_all x1 -> x0, blocking collectives: 26.3 us -> none  [local(): lax.all_to_all(jnp.broadcast_to(own, (NZ, TILE, 2 * HD)), 'z', 0, 0, tile...]
    all_to_all x0 -> x1, waiting for transfers between devices: none -> 16.1 us  [local(): lax.all_to_all(jnp.broadcast_to(own, (NZ, TILE, 2 * HD)), 'z', 0, 0, tile...]
    all_to_all x0 -> x1, starting transfers between devices: none -> 10.3 us  [local(): lax.all_to_all(jnp.broadcast_to(own, (NZ, TILE, 2 * HD)), 'z', 0, 0, tile...]
    ppermute x3, waiting for transfers between devices: 8.76 us -> 14.3 us  [along(): return lax.ppermute(a, ('x', 'c'), pairs)]
    all_to_all x1, waiting for transfers between devices: 4.28 us -> 0.01 us  [local(): q = lax.all_to_all(q, 't', 0, 0, tiled=True).reshape(TILE, GROUP * HD)]
    unnamed x10 -> x14, local copies, waits for them, and re-layouts: 2.5 us -> 3.71 us
    pallas_call x1 -> x2, Pallas kernels: 12.6 us -> 13.2 us  [the longest x1 9.41 us: first(): pl.pallas_call(functools.partial(first_kernel, base), out_shape=STATE, in...]
  transfers between devices with their start and end apart: 8 -> 9, of which waited for: 3 -> 3; matrix products, arithmetic and copies ran while one was open for 1% -> 1% of each run, Pallas kernels for 0% -> 8%
where the time goes in v5:
time: 112 us; the launch traced here: 111 us
  blocking collectives  33.9 us (30%)
  waiting for transfers between devices  30.3 us (27%)
  starting transfers between devices  25.8 us (23%)
  Pallas kernels  14.7 us (13%)
  local copies, waits for them, and re-layouts  6.08 us (5%)
    all_to_all x1, blocking collectives, local(): lax.all_to_all(out.reshape(NT, rows, GROUP * HD), 't', 0, 0, tiled=True)  18.5 us
    all_to_all x1, waiting for transfers between devices, local(): lax.all_to_all(jnp.broadcast_to(own, (NZ, TILE, 2 * HD)), 'z', 0, 0, tile...  16.1 us
    all_to_all x1, blocking collectives, local(): lax.all_to_all(spread(keys, values), 't', 0, 0, tiled=True)  15.5 us
    ppermute x3, waiting for transfers between devices, along(): return lax.ppermute(a, ('x', 'c'), pairs)  14.3 us
    all_to_all x1, starting transfers between devices, local(): lax.all_to_all(jnp.broadcast_to(own, (NZ, TILE, 2 * HD)), 'z', 0, 0, tile...  10.3 us
    pallas_call x1, Pallas kernels, first(): pl.pallas_call(functools.partial(first_kernel, base), out_shape=STATE, in...  9.41 us
    ppermute x3, starting transfers between devices, flip_from(): return lax.ppermute(a, ('x', 'c'), pairs)  6.24 us
    ppermute x3, starting transfers between devices, along(): return lax.ppermute(a, ('x', 'c'), pairs)  3.86 us
  transfers between devices with their start and end apart: 9, of which 3 were waited for; matrix products, arithmetic and copies ran while one was open for 1% of the time, Pallas kernels for 8%

profile of v5, /device:TPU:6, one launch (start us, length us, event | category | flops | bytes accessed | tf_op | source)
XLA Modules:
  0.0 111.2 jit_solution(18228164562147040917)
XLA Ops:
  0.0 1.5 %shard_map.55 = bf16[8,16,256]{2,1,0:T(8,128)(2,1)} custom-call(bf16[16,1024]{1,0:T(8,128)(2,1)} %k.1, bf16[16,1024]{1,0:T(8,128)(2,1)} %v.1), custom_call_target="tpu_custom_call" | custom-call | flops 1 | bytes 1 | tf_op jit(solution)/shard_map/pallas_call | solution.py:209
  1.5 15.5 %all_to_all.20 = bf16[8,16,256]{2,1,0:T(8,128)(2,1)S(1)} all-to-all(bf16[8,16,256]{2,1,0:T(8,128)(2,1)} %shard_map.55), channel_id=1, replica_groups=mesh['x'=4,'z'=8,'c'=2,'t'=8] {'t'}, dimensions={0} | all-to-all | bytes 131072 | tf_op jit(solution)/shard_map/all_to_all | solution.py:222
  17.0 0.8 broadcast_in_dim.50
  17.8 10.3 %all-to-all-start.1 = ((bf16[8,128,256]{2,1,0:T(8,128)(2,1)}), bf16[8,128,256]{2,1,0:T(8,128)(2,1)S(1)}, u32[]{:S(2)}, u32[]{:S(2)}) async-start(bf16[8,128,256]{2,1,0:T(8,128)(2,1)} %broadcast_in_dim.50), calls=%async_computation.1 | async-start | bytes 1048576 | tf_op jit(solution)/shard_map/all_to_all | solution.py:223
  28.1 16.1 %all-to-all-done.1.refs_0_ = bf16[8,128,256]{2,1,0:T(8,128)(2,1)S(1)} async-done(((bf16[8,128,256]{2,1,0:T(8,128)(2,1)}), bf16[8,128,256]{2,1,0:T(8,128)(2,1)S(1)}, u32[]{:S(2)}, u32[]{:S(2)}) %all-to-all-start.1) | async-done | bytes 524320 | tf_op jit(solution)/shard_map/all_to_all | solution.py:223
  44.2 1.9 %collective-permute-start = (bf16[8,128,256]{2,1,0:T(8,128)(2,1)S(1)}, bf16[8,128,256]{2,1,0:T(8,128)(2,1)S(1)}, u32[]{:S(2)}, u32[]{:S(2)}) collective-permute-start(bf16[8,128,256]{2,1,0:T(8,128)(2,1)S(1)} %all-to-all-done.1.refs_0_), channel_id=1, source_target_pairs={{0,8},{8,0},{1,9},{9,1},{2,10},{10,2},{3,11},{11,3},{4,12},{12,4},... | collective-permute-start | bytes 1572872 | tf_op jit(solution)/shard_map/ppermute | solution.py:162
  46.1 1.3 %collective-permute-start.1 = (bf16[8,128,256]{2,1,0:T(8,128)(2,1)S(1)}, bf16[8,128,256]{2,1,0:T(8,128)(2,1)S(1)}, u32[]{:S(2)}, u32[]{:S(2)}) collective-permute-start(bf16[8,128,256]{2,1,0:T(8,128)(2,1)S(1)} %all-to-all-done.1.refs_0_), channel_id=1, source_target_pairs={{0,128},{8,392},{128,256},{136,8},{256,384},{1,129},{9,393},{129,2... | collective-permute-start | bytes 1572872 | tf_op jit(solution)/shard_map/ppermute | solution.py:172
  47.4 1.3 %collective-permute-start.3 = (bf16[8,128,256]{2,1,0:T(8,128)(2,1)S(1)}, bf16[8,128,256]{2,1,0:T(8,128)(2,1)S(1)}, u32[]{:S(2)}, u32[]{:S(2)}) collective-permute-start(bf16[8,128,256]{2,1,0:T(8,128)(2,1)S(1)} %all-to-all-done.1.refs_0_), channel_id=1, source_target_pairs={{0,384},{8,136},{136,264},{264,392},{1,385},{9,137},{137,265},{265... | collective-permute-start | bytes 1572872 | tf_op jit(solution)/shard_map/ppermute | solution.py:172
  48.7 0.1 compare_reduce_fusion
  48.8 0.8 copy.13
  49.6 0.1 select_reduce_fusion.eff
  49.7 0.0 collective-permute-done.refs_1_
  49.7 3.5 %all-to-all-start.2 = ((bf16[8,16,1536]{2,1,0:T(8,128)(2,1)}), bf16[8,16,1536]{2,1,0:T(8,128)(2,1)S(1)}, u32[]{:S(2)}, u32[]{:S(2)}) async-start(bf16[8,16,1536]{2,1,0:T(8,128)(2,1)} %bitcast.13), calls=%async_computation.2 | async-start | bytes 786432 | tf_op jit(solution)/shard_map/all_to_all | solution.py:232
  53.2 8.8 %collective-permute-done.1.refs_2_ = bf16[8,128,256]{2,1,0:T(8,128)(2,1)S(1)} collective-permute-done((bf16[8,128,256]{2,1,0:T(8,128)(2,1)S(1)}, bf16[8,128,256]{2,1,0:T(8,128)(2,1)S(1)}, u32[]{:S(2)}, u32[]{:S(2)}) %collective-permute-start.1) | collective-permute-done | bytes 524320 | tf_op jit(solution)/shard_map/ppermute | solution.py:172
  62.0 1.3 %collective-permute-start.5 = (bf16[8,128,256]{2,1,0:T(8,128)(2,1)S(1)}, bf16[8,128,256]{2,1,0:T(8,128)(2,1)S(1)}, u32[]{:S(2)}, u32[]{:S(2)}) collective-permute-start(bf16[8,128,256]{2,1,0:T(8,128)(2,1)S(1)} %collective-permute-done.1.refs_2_), channel_id=1, source_target_pairs={{8,392},{128,256},{256,384},{392,264},{9,393},{129,257},{257,385},... | collective-permute-start | bytes 1572872 | tf_op jit(solution)/shard_map/ppermute | solution.py:172
  63.3 2.3 %collective-permute-start.2 = (bf16[8,128,256]{2,1,0:T(8,128)(2,1)S(1)}, bf16[8,128,256]{2,1,0:T(8,128)(2,1)S(1)}, u32[]{:S(2)}, u32[]{:S(2)}) collective-permute-start(bf16[8,128,256]{2,1,0:T(8,128)(2,1)S(1)} %collective-permute-done.1.refs_2_), channel_id=1, source_target_pairs={{128,136},{136,128},{256,264},{264,256},{384,392},{392,384},{129,1... | collective-permute-start | bytes 1572872 | tf_op jit(solution)/shard_map/ppermute | solution.py:177
  65.7 0.0 collective-permute-done.3.refs_4_
  65.7 2.0 %collective-permute-start.4 = (bf16[8,128,256]{2,1,0:T(8,128)(2,1)S(1)}, bf16[8,128,256]{2,1,0:T(8,128)(2,1)S(1)}, u32[]{:S(2)}, u32[]{:S(2)}) collective-permute-start(bf16[8,128,256]{2,1,0:T(8,128)(2,1)S(1)} %collective-permute-done.3.refs_4_), channel_id=1, source_target_pairs={{128,136},{136,128},{256,264},{264,256},{384,392},{392,384},{129,1... | collective-permute-start | bytes 1572872 | tf_op jit(solution)/shard_map/ppermute | solution.py:177
  67.6 5.4 %collective-permute-done.5.refs_0_ = bf16[8,128,256]{2,1,0:T(8,128)(2,1)S(1)} collective-permute-done((bf16[8,128,256]{2,1,0:T(8,128)(2,1)S(1)}, bf16[8,128,256]{2,1,0:T(8,128)(2,1)S(1)}, u32[]{:S(2)}, u32[]{:S(2)}) %collective-permute-start.5) | collective-permute-done | bytes 524320 | tf_op jit(solution)/shard_map/ppermute | solution.py:172
  73.1 1.9 %collective-permute-start.6 = (bf16[8,128,256]{2,1,0:T(8,128)(2,1)S(1)}, bf16[8,128,256]{2,1,0:T(8,128)(2,1)}, u32[]{:S(2)}, u32[]{:S(2)}) collective-permute-start(bf16[8,128,256]{2,1,0:T(8,128)(2,1)S(1)} %collective-permute-done.5.refs_0_), channel_id=1, source_target_pairs={{256,264},{264,256},{384,392},{392,384},{257,265},{265,257},{385,3... | collective-permute-start | bytes 1572872 | tf_op jit(solution)/shard_map/ppermute | solution.py:177
  75.0 0.0 collective-permute-done.2.refs_3_
  75.0 0.8 copy-done
  75.8 0.0 collective-permute-done.4.refs_5_
  75.8 0.8 copy-done.2
  76.6 0.0 all-to-all-done.2
  76.6 1.0 copy-done.1
  77.7 1.0 copy-done.3
  78.7 9.4 %shard_map.56 = (f32[12,128,128]{2,1,0:T(8,128)S(1)}, f32[12,128,256]{2,1,0:T(8,128)S(1)}) custom-call(s32[72]{0:T(128)S(1)} %select_reduce_fusion.eff, bf16[128,1536]{1,0:T(8,128)(2,1)S(1)} %bitcast.14, bf16[128,256]{1,0:T(8,128)(2,1)S(1)} %bitcast.18, bf16[8,128,256]{2,1,0:T(8,128)(2,1)S(1)} %all-to-all-done.1.refs_0_, ...), custom_call_target="tpu_custom_call" | custom-call | flops 6000000000 | bytes 1024 | tf_op jit(solution)/shard_map/pallas_call | solution.py:138
  88.1 0.0 collective-permute-done.6.refs_1_
  88.1 3.8 %shard_map.57 = bf16[128,1536]{1,0:T(8,128)(2,1)S(1)} custom-call(s32[72]{0:T(128)S(1)} %select_reduce_fusion.eff, bf16[128,1536]{1,0:T(8,128)(2,1)S(1)} %bitcast.15, f32[12,128,128]{2,1,0:T(8,128)S(1)} %get-tuple-element.13.m_in, f32[12,128,256]{2,1,0:T(8,128)S(1)} %get-tuple-element.14.acc_in, bf16[8,128,256]{2,1,0:T(8,128)(2,1)S(1)} %collective-permute-done.5.refs_0_, ...), custom_call_target="tpu_custom_call" | custom-call | flops 4000000000 | bytes 1024 | tf_op jit(solution)/shard_map/pallas_call | solution.py:150
  91.9 18.5 %all_to_all.21 = bf16[8,16,1536]{2,1,0:T(8,128)(2,1)S(1)} all-to-all(bf16[8,16,1536]{2,1,0:T(8,128)(2,1)S(1)} %bitcast.16), channel_id=1, replica_groups=mesh['x'=4,'z'=8,'c'=2,'t'=8] {'t'}, dimensions={0} | all-to-all | bytes 786432 | tf_op jit(solution)/shard_map/all_to_all | solution.py:240
  110.4 0.8 copy.11
  (12 shorter events, 0.0 us)
Async XLA Ops:
  0.0 48.7 %copy-start.6 = (s32[1,52]{1,0:T(1,128)S(1)}, s32[1,52]{1,0:T(1,128)}, u32[]{:S(2)}) copy-start(s32[1,52]{1,0:T(1,128)} %param.9) | copy-start | bytes 628
  0.0 48.8 %copy-start.4 = (bf16[16,12288]{1,0:T(8,128)(2,1)S(1)}, bf16[16,12288]{1,0:T(8,128)(2,1)}, u32[]{:S(2)}) copy-start(bf16[16,12288]{1,0:T(8,128)(2,1)} %param.5) | copy-start | bytes 1179652
  0.0 49.6 %copy-start.5 = (s32[64]{0:T(128)S(1)}, s32[64]{0:T(128)}, u32[]{:S(2)}) copy-start(s32[64]{0:T(128)} %param.8) | copy-start | bytes 772
  17.8 26.4 %all-to-all-start.1 = ((bf16[8,128,256]{2,1,0:T(8,128)(2,1)}), bf16[8,128,256]{2,1,0:T(8,128)(2,1)S(1)}, u32[]{:S(2)}, u32[]{:S(2)}) async-start(bf16[8,128,256]{2,1,0:T(8,128)(2,1)} %broadcast_in_dim.50), calls=%async_computation.1 | async-start | bytes 1048576 | tf_op jit(solution)/shard_map/all_to_all | solution.py:223
  44.2 5.5 %collective-permute-start = (bf16[8,128,256]{2,1,0:T(8,128)(2,1)S(1)}, bf16[8,128,256]{2,1,0:T(8,128)(2,1)S(1)}, u32[]{:S(2)}, u32[]{:S(2)}) collective-permute-start(bf16[8,128,256]{2,1,0:T(8,128)(2,1)S(1)} %all-to-all-done.1.refs_0_), channel_id=1, source_target_pairs={{0,8},{8,0},{1,9},{9,1},{2,10},{10,2},{3,11},{11,3},{4,12},{12,4},... | collective-permute-start | bytes 1572872 | tf_op jit(solution)/shard_map/ppermute | solution.py:162
  46.1 15.9 %collective-permute-start.1 = (bf16[8,128,256]{2,1,0:T(8,128)(2,1)S(1)}, bf16[8,128,256]{2,1,0:T(8,128)(2,1)S(1)}, u32[]{:S(2)}, u32[]{:S(2)}) collective-permute-start(bf16[8,128,256]{2,1,0:T(8,128)(2,1)S(1)} %all-to-all-done.1.refs_0_), channel_id=1, source_target_pairs={{0,128},{8,392},{128,256},{136,8},{256,384},{1,129},{9,393},{129,2... | collective-permute-start | bytes 1572872 | tf_op jit(solution)/shard_map/ppermute | solution.py:172
  47.4 18.2 %collective-permute-start.3 = (bf16[8,128,256]{2,1,0:T(8,128)(2,1)S(1)}, bf16[8,128,256]{2,1,0:T(8,128)(2,1)S(1)}, u32[]{:S(2)}, u32[]{:S(2)}) collective-permute-start(bf16[8,128,256]{2,1,0:T(8,128)(2,1)S(1)} %all-to-all-done.1.refs_0_), channel_id=1, source_target_pairs={{0,384},{8,136},{136,264},{264,392},{1,385},{9,137},{137,265},{265... | collective-permute-start | bytes 1572872 | tf_op jit(solution)/shard_map/ppermute | solution.py:172
  49.7 26.9 %all-to-all-start.2 = ((bf16[8,16,1536]{2,1,0:T(8,128)(2,1)}), bf16[8,16,1536]{2,1,0:T(8,128)(2,1)S(1)}, u32[]{:S(2)}, u32[]{:S(2)}) async-start(bf16[8,16,1536]{2,1,0:T(8,128)(2,1)} %bitcast.13), calls=%async_computation.2 | async-start | bytes 786432 | tf_op jit(solution)/shard_map/all_to_all | solution.py:232
  62.0 11.1 %collective-permute-start.5 = (bf16[8,128,256]{2,1,0:T(8,128)(2,1)S(1)}, bf16[8,128,256]{2,1,0:T(8,128)(2,1)S(1)}, u32[]{:S(2)}, u32[]{:S(2)}) collective-permute-start(bf16[8,128,256]{2,1,0:T(8,128)(2,1)S(1)} %collective-permute-done.1.refs_2_), channel_id=1, source_target_pairs={{8,392},{128,256},{256,384},{392,264},{9,393},{129,257},{257,385},... | collective-permute-start | bytes 1572872 | tf_op jit(solution)/shard_map/ppermute | solution.py:172
  63.3 11.7 %collective-permute-start.2 = (bf16[8,128,256]{2,1,0:T(8,128)(2,1)S(1)}, bf16[8,128,256]{2,1,0:T(8,128)(2,1)S(1)}, u32[]{:S(2)}, u32[]{:S(2)}) collective-permute-start(bf16[8,128,256]{2,1,0:T(8,128)(2,1)S(1)} %collective-permute-done.1.refs_2_), channel_id=1, source_target_pairs={{128,136},{136,128},{256,264},{264,256},{384,392},{392,384},{129,1... | collective-permute-start | bytes 1572872 | tf_op jit(solution)/shard_map/ppermute | solution.py:177
  65.7 10.1 %collective-permute-start.4 = (bf16[8,128,256]{2,1,0:T(8,128)(2,1)S(1)}, bf16[8,128,256]{2,1,0:T(8,128)(2,1)S(1)}, u32[]{:S(2)}, u32[]{:S(2)}) collective-permute-start(bf16[8,128,256]{2,1,0:T(8,128)(2,1)S(1)} %collective-permute-done.3.refs_4_), channel_id=1, source_target_pairs={{128,136},{136,128},{256,264},{264,256},{384,392},{392,384},{129,1... | collective-permute-start | bytes 1572872 | tf_op jit(solution)/shard_map/ppermute | solution.py:177
  73.1 15.1 %collective-permute-start.6 = (bf16[8,128,256]{2,1,0:T(8,128)(2,1)S(1)}, bf16[8,128,256]{2,1,0:T(8,128)(2,1)}, u32[]{:S(2)}, u32[]{:S(2)}) collective-permute-start(bf16[8,128,256]{2,1,0:T(8,128)(2,1)S(1)} %collective-permute-done.5.refs_0_), channel_id=1, source_target_pairs={{256,264},{264,256},{384,392},{392,384},{257,265},{265,257},{385,3... | collective-permute-start | bytes 1572872 | tf_op jit(solution)/shard_map/ppermute | solution.py:177
  75.0 0.8 copy-start
  75.8 0.8 copy-start.2
  76.6 1.0 copy-start.1
  77.7 1.0 copy-start.3
